TPU v7x, 128 devices: a whole 4x4x4 slice. The times are simulated.
128 devices in a mesh: fsdp: 4 (over z), ctx: 32 (over x, y, core).
Axes of the slice: x: 4, y: 4, z: 4, core: 2. Of those that a mesh axis runs over, the one named last changes fastest.
Arguments:
- hidden: bfloat16 [16384, 1536], P(('fsdp', 'ctx')), may hold values from -6 to 6
- segments: int32 [16384], P(('fsdp', 'ctx')), may hold values from 0 to 3, as said below
- norm_gain: float32 [1536], replicated, may hold values from 0.5 to 8
- in_weight: bfloat16 [1536, 6448], P(('fsdp', 'ctx')), may hold values from -0.6 to 0.6
- conv_weight: float32 [4, 3328], replicated, may hold values from -3 to 3
- conv_bias: float32 [3328], replicated, may hold values from -3 to 3
- dt_bias: float32 [48], replicated, may hold values from -1 to 0.5
- a_log: float32 [48], replicated, may hold values from -14 to -2
- skip_scale: float32 [48], replicated, may hold values from 0.5 to 2
- gate_gain: float32 [3072], replicated, may hold values from 0.25 to 1.75
- out_weight: bfloat16 [1536, 3072], P(('fsdp', 'ctx')), may hold values from -0.109375 to 0.109375
- cotangent: bfloat16 [16384, 1536], P(('fsdp', 'ctx')), may hold values from -30 to 30
- in_momentum: float32 [1536, 6448], P(('fsdp', 'ctx')), may hold values from -1536 to 1536
- out_momentum: float32 [1536, 3072], P(('fsdp', 'ctx')), may hold values from -1536 to 1536
- vector_momentum: float32 [21392], replicated, may hold values from -80 to 80
Outputs:
- block_output: bfloat16 [16384, 1536], P(('fsdp', 'ctx'))
- input_grad: float32 [16384, 1536], P(('fsdp', 'ctx'))
- in_grad: float32 [1536, 6448], P(('fsdp', 'ctx'))
- in_momentum_new: float32 [1536, 6448], P(('fsdp', 'ctx'))
- in_weight_new: float32 [1536, 6448], P(('fsdp', 'ctx'))
- out_grad: float32 [1536, 3072], P(('fsdp', 'ctx'))
- out_momentum_new: float32 [1536, 3072], P(('fsdp', 'ctx'))
- out_weight_new: float32 [1536, 3072], P(('fsdp', 'ctx'))
- vector_grad: float32 [21392], replicated
- vector_momentum_new: float32 [21392], replicated
- vector_new: float32 [21392], replicated
Inputs may be any that keep to these rules, and one draw needn't show every extreme that they name: `segments`: within each sequence of 4096 positions the document numbers start at 0 and rise by one at each new document, never falling; there are 4 documents, each of 200 positions or more.
All inputs are finite; a program needn't handle non-finite values.
Results may differ from a plain program's by a relative error of at most 0.028.
Values may be sent and summed in bfloat16 or wider, within the bound.
No kernel may reach another device: no remote copies, remote signals or barrier semaphores. Data moves between devices by JAX's collectives and lax.ppermute only.
A program may use at most 320 MiB of HBM per device.

v0:
```python
import math

import jax
import jax.numpy as jnp
from jax import lax
from jax.experimental import pallas as pl
from jax.experimental.pallas import tpu as pltpu
from jax.sharding import Mesh, PartitionSpec as P

NS_STEPS = 5
EPSILON = 1e-05
NORM_FLOOR = 1e-07
POLY_FIRST = 3.4445
POLY_SECOND = -4.775
POLY_THIRD = 2.0315
MATRIX_MOMENTUM = 0.95
MATRIX_RATE = 0.5
VECTOR_MOMENTUM = 0.9
VECTOR_RATE = 0.05
HIGHEST = lax.Precision.HIGHEST
F32 = jnp.float32
BF16 = jnp.bfloat16

EVERY = ("z", "x", "y", "c")
TEAM = ("y", "c")
ROWS = ("z", "x")

D = 1536
H = 48
HEAD = 64
N = 128
E = 3072
PROJ = 6448
TAPS = 4
G = 8
HG = H // G
EG = E // G
BG = 2 * N // G
TOKENS = 1024
CHUNK = 128
PIECES = TOKENS // CHUNK
AT_ONCE = 4
STEPS = PIECES // AT_ONCE
SPAN = AT_ONCE * CHUNK
EDGE = 16
LANES = 128
VG = EG + 2 * N
IN_COLS = 2 * EG + LANES
BLOCK = IN_COLS + EG
FORWARD_COLS = EG + VG + LANES
LATE_COLS = EG + LANES
STATE_ROWS = N + 8
TILE = 256
AHEAD, KEEP, TAIL, GAIN, SEGMENT = 4, 9, 10, 11, 12


def dot(a, b, dims):
    return lax.dot_general(
        a.astype(BF16), b.astype(BF16), (dims, ((), ())), preferred_element_type=F32
    )


NN = ((1,), (0,))
NT = ((1,), (1,))
TN = ((0,), (0,))


def parts(value):
    top = value.astype(BF16)
    return top, (value - top.astype(F32)).astype(BF16)


def dot3(a, b, dims=NN):
    a_top, a_rest = parts(a)
    b_top, b_rest = parts(b)
    return dot(a_top, b_top, dims) + (dot(a_top, b_rest, dims) + dot(a_rest, b_top, dims))


def lane_of(shape):
    return lax.broadcasted_iota(jnp.int32, shape, 1)


def piece_rows(k, height=CHUNK):
    return pl.ds(k * height, height)


def widen(per_head):
    rows = per_head.shape[0]
    left = lane_of((rows, LANES)) < HEAD
    return jnp.concatenate(
        [
            jnp.where(
                left,
                jnp.broadcast_to(per_head[:, 2 * p : 2 * p + 1], (rows, LANES)),
                jnp.broadcast_to(per_head[:, 2 * p + 1 : 2 * p + 2], (rows, LANES)),
            )
            for p in range(HG // 2)
        ],
        axis=1,
    )


def head_sums(values, summer):
    top, rest = parts(values)
    return dot(top, summer, NN) + dot(rest, summer, NN)


def pair_lanes(p):
    return slice(p * LANES, (p + 1) * LANES)


def stacked_pair(values):
    left = lane_of(values.shape) < HEAD
    zero = jnp.zeros_like(values)
    return jnp.concatenate(
        [jnp.where(left, values, zero), jnp.where(left, zero, values)], axis=0
    )


def running(mask, values):
    top, rest = parts(values)
    least = values - top.astype(F32) - rest.astype(F32)
    return dot(mask, top, NN) + (dot(mask, rest, NN) + dot(mask, least, NN))


def silu_parts(values):
    sig = jax.nn.sigmoid(values)
    return sig, values * sig


def softplus(values):
    return jnp.maximum(values, 0.0) + jnp.log1p(jnp.exp(-jnp.abs(values)))


def square_iota():
    shape = (CHUNK, CHUNK)
    return lax.broadcasted_iota(jnp.int32, shape, 0), lane_of(shape)


def same_document(flags, row):
    return flags[:, SEGMENT : SEGMENT + 1] == row


def in_order(core_ref, own_ref, other_ref):
    own, other = own_ref[0], other_ref[0]
    first = core_ref[1] == 0
    return jnp.concatenate(
        [jnp.where(first, own, other), jnp.where(first, other, own)], axis=0
    )


def project_kernel(
    core_ref, own_ref, other_ref, edge_ref, w_ref, gain_ref, normed_ref, z_ref, v_ref, r_ref
):
    def put(x, at):
        x = x.astype(F32)
        scale = lax.rsqrt(jnp.mean(x * x, axis=1, keepdims=True) + EPSILON)
        normed = (x * scale * gain_ref[...]).astype(BF16)
        normed_ref[at, :] = normed
        out = jnp.dot(normed, w_ref[...], preferred_element_type=F32)
        z_ref[at, :] = out[:, :EG]
        v_ref[at, :] = out[:, EG : EG + VG]
        r_ref[at, :] = out[:, EG + VG :]

    last = pl.num_programs(0) - 1

    @pl.when(pl.program_id(0) < last)
    def _():
        put(in_order(core_ref, own_ref, other_ref), pl.ds(0, 2 * CHUNK))

    @pl.when(pl.program_id(0) == last)
    def _():
        put(edge_ref[...], pl.ds(0, EDGE))


def incoming_kernel(core_ref, own_ref, other_ref, w_ref, q_ref, d_gated_ref):
    q = in_order(core_ref, own_ref, other_ref)
    q_ref[...] = q
    d_gated_ref[...] = jnp.dot(q, w_ref[...], preferred_element_type=F32)


def early_kernel(normed_ref, q_ref, dz_ref, gated_ref, out_ref):
    out_ref[:, :EG] = dot(normed_ref[0:TOKENS, :], dz_ref[...], TN).astype(BF16)
    out_ref[:, EG:] = dot(q_ref[...], gated_ref[...], TN).astype(BF16)


def forward_kernel(
    v_ref,
    before_ref,
    r_ref,
    flags_ref,
    ids_ref,
    taps_ref,
    head_ref,
    conv_ref,
    dt_ref,
    cum_ref,
    y_ref,
    start_ref,
    reach_ref,
    gain_ref,
    packed_ref,
    state,
    reach,
):
    step = pl.program_id(0)

    @pl.when(step == 0)
    def _():
        state[...] = jnp.zeros_like(state)
        reach[...] = jnp.ones_like(reach)

    for k in range(AT_ONCE):
        c = step * AT_ONCE + k
        at, at8 = piece_rows(k), piece_rows(k, 8)
        flags = flags_ref[at, :]
        window = jnp.concatenate([before_ref[...] if k == 0 else v_ref[pl.ds(k * CHUNK - 8, 8), :], v_ref[at, :]], axis=0)
        conv = taps_ref[TAPS : TAPS + 1, :] + taps_ref[0:1, :] * window[8:]
        for lag in range(1, TAPS):
            conv = conv + taps_ref[lag : lag + 1, :] * (
                pltpu.roll(window, lag, 0)[8:] * flags[:, lag : lag + 1]
            )
        conv_ref[at, :] = conv
        act = conv * jax.nn.sigmoid(conv)
        xs, bm, cm = act[:, :EG], act[:, EG : EG + N], act[:, EG + N :]
        dt = softplus(r_ref[at, :] + head_ref[0:1, :])
        dt_ref[at, :] = dt
        ti, si = square_iota()
        lower = (ti >= si).astype(F32)
        cum = running(lower, -head_ref[1:2, :] * dt)
        cum_ref[at, :] = cum
        cum_t = cum.T
        last = cum[CHUNK - 1 : CHUNK, :]
        tail = jnp.exp(last - cum) * flags[:, TAIL : TAIL + 1]
        carry = jnp.exp(cum) * flags[:, KEEP : KEEP + 1]
        gain = widen(jnp.exp(last) * flags[0:1, GAIN : GAIN + 1])
        xdt = xs * widen(dt)
        scores = dot3(cm, bm, NT)
        mask = (ti >= si) & same_document(flags, ids_ref[pl.ds(c, 1), :])
        within = []
        for p in range(HG // 2):
            mix = [
                jnp.exp(jnp.where(mask, cum[:, h : h + 1] - cum_t[h : h + 1, :], -1e30)) * scores
                for h in (2 * p, 2 * p + 1)
            ]
            within.append(
                dot3(jnp.concatenate(mix, axis=1), stacked_pair(xdt[:, pair_lanes(p)]))
            )
        y_ref[at, :] = jnp.concatenate(within, axis=1) + widen(carry) * dot3(cm, state[...])
        start_ref[k] = state[...]
        reach_ref[at8, :] = reach[...]
        gain_ref[at8, :] = jnp.broadcast_to(gain, (8, EG))
        state[...] = gain * state[...] + dot3(bm.T, xdt * widen(tail))
        reach[...] = gain * reach[...]

    @pl.when(step == STEPS - 1)
    def _():
        packed_ref[0:N, :] = state[...]
        packed_ref[N:, :] = reach[...]


def joined_states(first, second, third):
    return first[:N] + first[N : N + 1] * (second[:N] + second[N : N + 1] * third[:N])


def output_kernel(
    y_part_ref,
    conv_ref,
    cum_ref,
    flags_ref,
    z_ref,
    d_gated_ref,
    reach_ref,
    first_ref,
    second_ref,
    third_ref,
    rows_ref,
    y_ref,
    sums_ref,
    arrived_ref,
):
    step = pl.program_id(0)

    @pl.when(step == 0)
    def _():
        arrived_ref[...] = joined_states(first_ref[...], second_ref[...], third_ref[...])

    for k in range(AT_ONCE):
        c = step * AT_ONCE + k
        at = piece_rows(k)
        conv = conv_ref[at, :]
        act = conv * jax.nn.sigmoid(conv)
        carry = widen(jnp.exp(cum_ref[at, :]) * flags_ref[at, KEEP : KEEP + 1]) * reach_ref[pl.ds(8 * k, 1), :]
        y = (
            y_part_ref[at, :]
            + carry * dot3(act[:, EG + N :], arrived_ref[...])
            + rows_ref[0:1, :] * act[:, :EG]
        )
        y_ref[at, :] = y
        _, silu_z = silu_parts(z_ref[at, :])
        g = y * silu_z
        squares = jnp.sum(g * g, axis=1, keepdims=True)
        inner = jnp.sum(d_gated_ref[at, :] * rows_ref[1:2, :] * g, axis=1, keepdims=True)
        lane = lane_of((CHUNK, LANES))
        turned = jnp.where(lane == 0, squares, jnp.where(lane == 1, inner, 0.0)).T
        sums_ref[pl.ds(c, 1), :] = turned[0:1, :]
        sums_ref[pl.ds(PIECES + c, 1), :] = turned[1:2, :]


def gate_kernel(
    y_ref,
    z_ref,
    d_gated_ref,
    conv_ref,
    cum_ref,
    flags_ref,
    gain_ref,
    sums_ref,
    rows_ref,
    gated_ref,
    dz_ref,
    dy_ref,
    end_ref,
    reach_ref,
    d_gate_ref,
    packed_ref,
    state,
    reach,
):
    step = STEPS - 1 - pl.program_id(0)

    @pl.when(step == STEPS - 1)
    def _():
        state[...] = jnp.zeros_like(state)
        reach[...] = jnp.ones_like(reach)
        d_gate_ref[...] = jnp.zeros_like(d_gate_ref)

    for k in reversed(range(AT_ONCE)):
        c = step * AT_ONCE + k
        at, at8 = piece_rows(k), piece_rows(k, 8)
        ti, _ = square_iota()
        turned = jnp.where(
            ti == 0,
            sums_ref[pl.ds(c, 1), :],
            jnp.where(ti == 1, sums_ref[pl.ds(PIECES + c, 1), :], 0.0),
        ).T
        root = lax.rsqrt(turned[:, 0:1] * (1.0 / E) + EPSILON)
        slope = turned[:, 1:2] * (root * root * root) * (1.0 / E)
        gate = rows_ref[1:2, :]
        y = y_ref[at, :]
        sig, silu_z = silu_parts(z_ref[at, :])
        g = y * silu_z
        unit = g * root
        gated_ref[at, :] = (unit * gate).astype(BF16)
        d_gated = d_gated_ref[at, :]
        d_gate_ref[0:1, :] += jnp.sum(d_gated * unit, axis=0, keepdims=True)
        d_g = root * (d_gated * gate) - g * slope
        dy = d_g * silu_z
        dz_ref[at, :] = (d_g * y * (sig + silu_z * (1.0 - sig))).astype(BF16)
        dy_ref[at, :] = dy
        conv = conv_ref[at, EG + N :]
        cm = conv * jax.nn.sigmoid(conv)
        carry = widen(jnp.exp(cum_ref[at, :]) * flags_ref[at, KEEP : KEEP + 1])
        end_ref[k] = state[...]
        reach_ref[at8, :] = reach[...]
        gain = gain_ref[pl.ds(8 * k, 1), :]
        state[...] = gain * state[...] + dot3(cm.T, dy * carry)
        reach[...] = gain * reach[...]

    @pl.when(step == 0)
    def _():
        packed_ref[0:N, :] = state[...]
        packed_ref[N:, :] = reach[...]


def inner_kernel(dy_ref, conv_ref, dt_ref, cum_ref, flags_ref, ids_ref, u_ref, d_bc_ref):
    for k in range(AT_ONCE):
        c = pl.program_id(0) * AT_ONCE + k
        at = piece_rows(k)
        flags = flags_ref[at, :]
        conv = conv_ref[at, :]
        act = conv * jax.nn.sigmoid(conv)
        xs, bm, cm = act[:, :EG], act[:, EG : EG + N], act[:, EG + N :]
        cum = cum_ref[at, :]
        cum_t = cum.T
        dy = dy_ref[at, :]
        xdt = xs * widen(dt_ref[at, :])
        scores_t = dot3(bm, cm, NT)
        ti, si = square_iota()
        same = same_document(flags, ids_ref[pl.ds(c, 1), :])
        mask = (ti >= si) & same
        mask_t = (ti <= si) & same
        d_scores = jnp.zeros((CHUNK, CHUNK), F32)
        u = []
        for p in range(HG // 2):
            own = stacked_pair(dy[:, pair_lanes(p)])
            pairs = dot3(own, xdt[:, pair_lanes(p)], NT)
            mix_t = []
            for k in range(2):
                h = 2 * p + k
                gap = cum[:, h : h + 1] - cum_t[h : h + 1, :]
                d_scores = d_scores + jnp.exp(jnp.where(mask, gap, -1e30)) * (
                    pairs[k * CHUNK : (k + 1) * CHUNK]
                )
                mix_t.append(jnp.exp(jnp.where(mask_t, -gap, -1e30)) * scores_t)
            u.append(dot(jnp.concatenate(mix_t, axis=1), own, NN))
        u_ref[at, :] = jnp.concatenate(u, axis=1)
        d_bc_ref[at, :N] = dot3(d_scores.T, cm)
        d_bc_ref[at, N:] = dot3(d_scores, bm)


def backward_kernel(
    core_ref,
    u_ref,
    d_bc_ref,
    dy_ref,
    y_ref,
    conv_ref,
    dt_ref,
    cum_ref,
    r_ref,
    flags_ref,
    start_ref,
    reach_ref,
    arrived_ref,
    end_ref,
    reach_back_ref,
    first_ref,
    second_ref,
    third_ref,
    final_ref,
    v_ref,
    before_ref,
    rows_ref,
    taps_ref,
    head_ref,
    summer_ref,
    edge_flags_ref,
    dv_ref,
    d_edge_ref,
    kept_ref,
    sent_ref,
    dr_ref,
    wide_ref,
    heads_ref,
    following,
    flowing,
    adjoint_in,
):
    step = STEPS - 1 - pl.program_id(0)
    summer = summer_ref[...]

    @pl.when(step == STEPS - 1)
    def _():
        adjoint = joined_states(first_ref[...], second_ref[...], third_ref[...])
        adjoint_in[...] = adjoint
        final = final_ref[0:N, :] + final_ref[N : N + 1, :] * arrived_ref[...]
        inner = jnp.sum(adjoint * final, axis=0, keepdims=True)
        flowing[...] = head_sums(jnp.broadcast_to(inner, (8, EG)), summer)
        following[...] = jnp.zeros_like(following)
        wide_ref[...] = jnp.zeros_like(wide_ref)
        heads_ref[...] = jnp.zeros_like(heads_ref)

    for k in reversed(range(AT_ONCE)):
        at = piece_rows(k)
        flags = flags_ref[at, :]
        conv = conv_ref[at, :]
        sig, act = silu_parts(conv)
        xs, bm = act[:, :EG], act[:, EG : EG + N]
        cum = cum_ref[at, :]
        dt = dt_ref[at, :]
        dy = dy_ref[at, :]
        skip = rows_ref[0:1, :]
        rate = head_ref[1:2, :]
        last = cum[CHUNK - 1 : CHUNK, :]
        tail = widen(jnp.exp(last - cum) * flags[:, TAIL : TAIL + 1])
        carry = widen(jnp.exp(cum) * flags[:, KEEP : KEEP + 1])
        dt_wide = widen(dt)
        start = start_ref[k] + reach_ref[pl.ds(8 * k, 1), :] * arrived_ref[...]
        adjoint = end_ref[k] + reach_back_ref[pl.ds(8 * k, 1), :] * adjoint_in[...]
        u = u_ref[at, :] + tail * dot3(bm, adjoint)
        d_xs = u * dt_wide + skip * dy
        d_dt = head_sums(xs * u, summer)
        d_bm = d_bc_ref[at, :N] + dot3(xs * dt_wide * tail, adjoint, NT)
        d_cm = d_bc_ref[at, N:] + dot3(dy * carry, start, NT)
        turned = jnp.concatenate([d_bm.T, d_cm.T], axis=0)
        of_core = [
            jnp.concatenate(
                [turned[(2 * y + c) * BG : (2 * y + c + 1) * BG] for y in range(G // 2)], axis=0
            )
            for c in range(2)
        ]
        first = core_ref[1] == 0
        kept_ref[:, at] = jnp.where(first, of_core[0], of_core[1])
        sent_ref[:, at] = jnp.where(first, of_core[1], of_core[0])
        flow = head_sums(dy * (y_ref[at, :] - skip * xs), summer) - dt * d_dt
        ti, si = square_iota()
        upper = (si >= ti).astype(F32)
        d_la = running(upper, flow) + flowing[0:1, :]
        flowing[...] = jnp.broadcast_to(d_la[0:1, :], flowing.shape)
        d_la = d_la * flags[:, 1:2]
        d_r = (d_dt - rate * d_la) * jax.nn.sigmoid(r_ref[at, :] + head_ref[0:1, :])
        dr_ref[at, :] = d_r
        heads_ref[0:1, :] += jnp.sum(d_r, axis=0, keepdims=True)
        heads_ref[1:2, :] += jnp.sum(d_la * (-rate * dt), axis=0, keepdims=True)
        heads_ref[2:3, :] += jnp.sum(head_sums(dy * xs, summer), axis=0, keepdims=True)

        sig, conv = sig[:, :EG], conv[:, :EG]
        d_conv = d_xs * (sig + conv * sig * (1.0 - sig))
        window = jnp.concatenate([before_ref[...] if k == 0 else v_ref[pl.ds(k * CHUNK - 8, 8), :], v_ref[at, :]], axis=0)
        ahead = jnp.concatenate([d_conv, following[...]], axis=0)
        wide_ref[0:1, :] += jnp.sum(d_conv * window[8:], axis=0, keepdims=True)
        wide_ref[TAPS : TAPS + 1, :] += jnp.sum(d_conv, axis=0, keepdims=True)
        dv = taps_ref[0:1, :EG] * d_conv
        for lag in range(1, TAPS):
            wide_ref[lag : lag + 1, :] += jnp.sum(
                d_conv * pltpu.roll(window, lag, 0)[8:] * flags[:, lag : lag + 1],
                axis=0,
                keepdims=True,
            )
            dv = dv + taps_ref[lag : lag + 1, :EG] * (
                pltpu.roll(ahead, CHUNK + 8 - lag, 0)[:CHUNK] * flags[:, AHEAD + lag : AHEAD + lag + 1]
            )
        dv_ref[at, :] = dv.astype(BF16)
        following[...] = d_conv[0:8]

    @pl.when(step == 0)
    def _():
        d_edge_ref[...] = edge_rows(following[...], taps_ref[:, :EG], edge_flags_ref[...])


def edge_rows(d_conv, taps, flags):
    zero = jnp.zeros_like(d_conv)
    ahead = jnp.concatenate([zero, d_conv], axis=0)
    total = zero
    for lag in range(1, TAPS):
        total = total + taps[lag : lag + 1, :] * (
            pltpu.roll(ahead, EDGE - lag, 0)[0:8] * flags[:, AHEAD + lag : AHEAD + lag + 1]
        )
    return jnp.concatenate([zero, total], axis=0).astype(BF16)


def shared_kernel(
    team_ref,
    got_refs,
    conv_b_ref,
    conv_c_ref,
    v_b_ref,
    v_c_ref,
    before_b_ref,
    before_c_ref,
    dr_ref,
    dv_ref,
    d_edge_ref,
    flags_ref,
    edge_flags_ref,
    taps_ref,
    late_ref,
    wide_ref,
    following,
):
    step = pl.program_id(0)
    turn = (2 * N - BG * team_ref[0]) % (2 * N)

    def own(b, c):
        return pltpu.roll(jnp.concatenate([b, c], axis=1), turn, 1)[:, :LANES]

    def before(k):
        if k == 0:
            return own(before_b_ref[...], before_c_ref[...])
        last = pl.ds(k * CHUNK - 8, 8)
        return own(v_b_ref[last, :], v_c_ref[last, :])

    @pl.when(step == 0)
    def _():
        following[...] = jnp.zeros_like(following)
        wide_ref[...] = jnp.zeros_like(wide_ref)

    def piece(k):
        at = piece_rows(k)
        flags = flags_ref[at, :]
        total = sum(ref[:, at] for ref in got_refs)
        d_act = jnp.concatenate([total, jnp.zeros((LANES - BG, CHUNK), F32)], axis=0).T
        conv = own(conv_b_ref[at, :], conv_c_ref[at, :])
        sig = jax.nn.sigmoid(conv)
        d_conv = d_act * (sig + conv * sig * (1.0 - sig))
        window = jnp.concatenate(
            [before(k), own(v_b_ref[at, :], v_c_ref[at, :])], axis=0
        )
        ahead = jnp.concatenate([d_conv, following[...]], axis=0)
        wide_ref[0:1, :] += jnp.sum(d_conv * window[8:], axis=0, keepdims=True)
        wide_ref[TAPS : TAPS + 1, :] += jnp.sum(d_conv, axis=0, keepdims=True)
        dv = taps_ref[0:1, :] * d_conv
        for lag in range(1, TAPS):
            wide_ref[lag : lag + 1, :] += jnp.sum(
                d_conv * pltpu.roll(window, lag, 0)[8:] * flags[:, lag : lag + 1],
                axis=0,
                keepdims=True,
            )
            dv = dv + taps_ref[lag : lag + 1, :] * (
                pltpu.roll(ahead, CHUNK + 8 - lag, 0)[:CHUNK]
                * flags[:, AHEAD + lag : AHEAD + lag + 1]
            )
        following[...] = d_conv[0:8]
        late_ref[at, :EG] = dv_ref[at, :]
        late_ref[at, EG:] = (dv + pltpu.roll(dr_ref[at, :], BG, 1)).astype(BF16)

    @pl.when(step < STEPS)
    def _():
        for k in reversed(range(AT_ONCE)):
            piece(k)

    @pl.when(step == STEPS)
    def _():
        late_ref[0:EDGE, :EG] = d_edge_ref[...]
        late_ref[0:EDGE, EG:] = edge_rows(following[...], taps_ref[...], edge_flags_ref[...])


def triangle(n):
    return [(i, j) for i in range(n // TILE) for j in range(i, n // TILE)]


def gram_kernel(which_ref, x_ref, out_ref, held, total, in_sems, out_sems):
    parts_of_x, n, _ = x_ref.shape
    count = n // TILE
    order = triangle(n)

    def at(i):
        return pl.ds(i * TILE, TILE)

    def run(columns):
        width = columns.stop - columns.start
        arriving = [
            pltpu.make_async_copy(
                x_ref.at[y, :, columns], held.at[y, :, pl.ds(0, width)], in_sems.at[y]
            )
            for y in range(parts_of_x)
        ]
        leaving = []
        for copy in arriving:
            copy.start()
        for y in range(0, parts_of_x, 2):
            for copy in (arriving[y], arriving[y + 1]):
                copy.wait()
            for i in range(count):

                def taken(rows):
                    return jnp.concatenate(
                        [held[y, rows, :width], held[y + 1, rows, :width]], axis=1
                    )

                product = dot(taken(at(i)), taken(pl.ds(i * TILE, n - i * TILE)), NT)
                own = order.index((i, i))
                for j in range(i, count):
                    block = product[:, (j - i) * TILE : (j - i + 1) * TILE]
                    b = own + j - i
                    total[b] = block if y == 0 else total[b] + block
                if y + 2 == parts_of_x:
                    blocks = pl.ds(own, count - i)
                    leaving.append(
                        pltpu.make_async_copy(
                            total.at[blocks], out_ref.at[blocks], out_sems.at[i]
                        )
                    )
                    leaving[-1].start()
        for copy in leaving:
            copy.wait()

    @pl.when(which_ref[0] == 1)
    def _():
        run(slice(0, IN_COLS))

    @pl.when(which_ref[0] != 1)
    def _():
        run(slice(IN_COLS, BLOCK))


def chain_kernel(own_ref, got_ref, pick_ref, t_ref, high, low, h_high, h_low, q_ref):
    n = high.shape[0]
    count = n // TILE
    order = triangle(n)

    def at(i):
        return pl.ds(i * TILE, TILE) if isinstance(i, int) else pl.ds(pl.multiple_of(i * TILE, TILE), TILE)

    def times(a, b):
        return jnp.dot(a, b, preferred_element_type=F32)

    diagonal = lax.broadcasted_iota(jnp.int32, (TILE, TILE), 0) == lax.broadcasted_iota(jnp.int32, (TILE, TILE), 1)
    square = jnp.zeros((1, 1), F32)
    for b, (i, j) in enumerate(order):
        if i == j:
            square = square + jnp.sum(jnp.where(diagonal, own_ref[b] + got_ref[b], 0.0), keepdims=True)
    inverse = 1.0 / (jnp.sqrt(square) + NORM_FLOOR)
    scale = inverse * inverse

    def put(value, i, j, top_ref, rest_ref):
        top = value.astype(BF16)
        top_ref[at(i), at(j)] = top
        if i != j:
            top_ref[at(j), at(i)] = top.T
        if rest_ref is not None:
            rest_ref[at(i), at(j)] = (value - top.astype(F32)).astype(BF16)

    def put_row(value, i, top_ref, rest_ref):
        for j in range(i, count):
            put(value[:, (j - i) * TILE : (j - i + 1) * TILE], i, j, top_ref, rest_ref)

    for b, (i, j) in enumerate(order):
        put((own_ref[b] + got_ref[b]) * scale, i, j, high, low)

    def polynomial(q):
        for i in range(count):
            rest = pl.ds(i * TILE, n - i * TILE)
            value = times(high[at(i), :], high[:, rest])
            put_row(POLY_SECOND * high[at(i), rest].astype(F32) + POLY_THIRD * value, i, q, None)

    def whole(top_ref, rest_ref, i, rest):
        return top_ref[at(i), rest].astype(F32) + rest_ref[at(i), rest].astype(F32)

    def iterate(step, _):
        q = q_ref.at[step]
        polynomial(q)
        for i in range(count):
            rest = pl.ds(i * TILE, n - i * TILE)
            value = times(q[at(i), :], high[:, rest]) + POLY_FIRST * whole(high, low, i, rest)
            put_row(value, i, h_high, h_low)
        for i in range(count):
            rest = pl.ds(i * TILE, n - i * TILE)
            value = times(h_high[at(i), :], q[:, rest]) + POLY_FIRST * whole(h_high, h_low, i, rest)
            put_row(value, i, high, low)
        return 0

    def thin(t, matrix):
        top, rest = parts(t)
        both = times(jnp.concatenate([top, rest], axis=0), matrix)
        return both[: t.shape[0]] + both[t.shape[0] :]

    def multiplied(t, step):
        return POLY_FIRST * t + thin(t, q_ref[step])

    def last_gram(t):
        return multiplied(thin(multiplied(t, NS_STEPS - 2), high[...]), NS_STEPS - 2)

    lax.fori_loop(0, NS_STEPS - 2, iterate, 0)
    polynomial(q_ref.at[NS_STEPS - 2])
    pick = pick_ref[...]
    once = last_gram(pick)
    t = POLY_FIRST * pick + POLY_SECOND * once + POLY_THIRD * last_gram(once)
    for step in reversed(range(NS_STEPS - 1)):
        t = multiplied(t, step)
    t_ref[...] = t * inverse


SMALL = pltpu.CompilerParams(vmem_limit_bytes=20 << 20)
LARGE = pltpu.CompilerParams(vmem_limit_bytes=60 << 20)


def spec(shape, index=None):
    return pl.BlockSpec(shape, index if index is not None else (lambda c: (0,) * len(shape)))


def rows(width, height=SPAN):
    return spec((height, width), lambda c: (c, 0))


def rows_back(width, height=SPAN):
    return spec((height, width), lambda c: (STEPS - 1 - c, 0))


def previous(c):
    return jnp.where(c == 0, (TOKENS + EDGE) // 8 - 1, c * (SPAN // 8) - 1)


def shaped(*shape, dtype=F32):
    return jax.ShapeDtypeStruct(shape, dtype)


def cost(flops, moved):
    return pl.CostEstimate(flops=flops, bytes_accessed=moved, transcendentals=0)


def piece_of(kind):
    size = 4

    def index(c, place):
        return ((place[0] - jnp.minimum(c, size - 1) + size) % size, 0, 0)

    return pl.BlockSpec((1, CHUNK, D), index)


def project(place, own, other, edge, weights, gain):
    total = TOKENS + EDGE
    block = 2 * CHUNK

    def out(width):
        return pl.BlockSpec((block, width), lambda c, place: (c, 0))

    def whole(*shape):
        return pl.BlockSpec(shape, lambda c, place: (0, 0))

    return pl.pallas_call(
        project_kernel,
        grid_spec=pltpu.PrefetchScalarGridSpec(
            num_scalar_prefetch=1,
            grid=(TOKENS // block + 1,),
            in_specs=[
                piece_of("own"),
                piece_of("other"),
                whole(EDGE, D),
                whole(D, FORWARD_COLS),
                whole(1, D),
            ],
            out_specs=[out(D), out(EG), out(VG), out(LANES)],
        ),
        out_shape=[
            shaped(total, D, dtype=BF16),
            shaped(total, EG),
            shaped(total, VG),
            shaped(total, LANES),
        ],
        compiler_params=SMALL,
        cost_estimate=cost(2 * total * D * FORWARD_COLS, 16 << 20),
        name="project",
    )(place, own, other, edge, weights, gain)


def incoming(place, own, other, weights):
    block = 2 * CHUNK

    def out(width):
        return pl.BlockSpec((block, width), lambda c, place: (c, 0))

    return pl.pallas_call(
        incoming_kernel,
        grid_spec=pltpu.PrefetchScalarGridSpec(
            num_scalar_prefetch=1,
            grid=(TOKENS // block,),
            in_specs=[
                piece_of("own"),
                piece_of("other"),
                pl.BlockSpec((D, EG), lambda c, place: (0, FORWARD_COLS // EG)),
            ],
            out_specs=[out(D), out(EG)],
        ),
        out_shape=[shaped(TOKENS, D, dtype=BF16), shaped(TOKENS, EG)],
        compiler_params=SMALL,
        cost_estimate=cost(2 * TOKENS * D * EG, 9 << 20),
        name="incoming",
    )(place, own, other, weights)


def early_products(normed, q, dz, gated):
    return pl.pallas_call(
        early_kernel,
        grid=(D // TILE,),
        in_specs=[
            spec((TOKENS + EDGE, TILE), lambda c: (0, c)),
            spec((TOKENS, TILE), lambda c: (0, c)),
            spec((TOKENS, EG)),
            spec((TOKENS, EG)),
        ],
        out_specs=rows(2 * EG, TILE),
        out_shape=shaped(D, 2 * EG, dtype=BF16),
        compiler_params=SMALL,
        cost_estimate=cost(4 * TOKENS * D * EG, 13 << 20),
        name="early",
    )(normed, q, dz, gated)


def forward(v, r, flags, ids, taps, head):
    return pl.pallas_call(
        forward_kernel,
        grid=(STEPS,),
        in_specs=[
            rows(VG),
            spec((8, VG), lambda c: (previous(c), 0)),
            rows(LANES),
            rows(LANES),
            spec((8, LANES)),
            spec((8, VG)),
            spec((8, LANES)),
        ],
        out_specs=[
            rows(VG),
            rows(LANES),
            rows(LANES),
            rows(EG),
            spec((AT_ONCE, N, EG), lambda c: (c, 0, 0)),
            rows(EG, 8 * AT_ONCE),
            rows(EG, 8 * AT_ONCE),
            spec((STATE_ROWS, EG)),
        ],
        out_shape=[
            shaped(TOKENS, VG),
            shaped(TOKENS, LANES),
            shaped(TOKENS, LANES),
            shaped(TOKENS, EG),
            shaped(PIECES, N, EG),
            shaped(PIECES * 8, EG),
            shaped(PIECES * 8, EG),
            shaped(STATE_ROWS, EG),
        ],
        scratch_shapes=[pltpu.VMEM((N, EG), F32), pltpu.VMEM((8, EG), F32)],
        compiler_params=SMALL,
        cost_estimate=cost(3 << 30, 14 << 20),
        name="forward",
    )(v, v, r, flags, ids, taps, head)


def outputs(y_part, conv, cum, flags, z, d_gated, reach, arrivals, wide):
    return pl.pallas_call(
        output_kernel,
        grid=(STEPS,),
        in_specs=[rows(EG), rows(VG), rows(LANES), rows(LANES), rows(EG), rows(EG), rows(EG, 8 * AT_ONCE)]
        + [spec((STATE_ROWS, EG))] * 3
        + [spec((8, EG))],
        out_specs=[rows(EG), spec((2 * PIECES, LANES)), spec((N, EG))],
        out_shape=[shaped(TOKENS, EG), shaped(2 * PIECES, LANES), shaped(N, EG)],
        compiler_params=SMALL,
        cost_estimate=cost(1 << 28, 12 << 20),
        name="outputs",
    )(y_part, conv, cum, flags, z, d_gated, reach, *arrivals, wide)


def gate(y, z, d_gated, conv, cum, flags, gain, sums, wide):
    return pl.pallas_call(
        gate_kernel,
        grid=(STEPS,),
        in_specs=[rows_back(EG)] * 3
        + [rows_back(VG), rows_back(LANES), rows_back(LANES), rows_back(EG, 8 * AT_ONCE)]
        + [spec((2 * PIECES, LANES)), spec((8, EG))],
        out_specs=[rows_back(EG)] * 3
        + [
            spec((AT_ONCE, N, EG), lambda c: (STEPS - 1 - c, 0, 0)),
            rows_back(EG, 8 * AT_ONCE),
            spec((8, EG)),
            spec((STATE_ROWS, EG)),
        ],
        out_shape=[
            shaped(TOKENS, EG, dtype=BF16),
            shaped(TOKENS, EG, dtype=BF16),
            shaped(TOKENS, EG),
            shaped(PIECES, N, EG),
            shaped(PIECES * 8, EG),
            shaped(8, EG),
            shaped(STATE_ROWS, EG),
        ],
        scratch_shapes=[pltpu.VMEM((N, EG), F32), pltpu.VMEM((8, EG), F32)],
        compiler_params=SMALL,
        cost_estimate=cost(1 << 28, 14 << 20),
        name="gate",
    )(y, z, d_gated, conv, cum, flags, gain, sums, wide)


def inner(dy, conv, dt, cum, flags, ids):
    return pl.pallas_call(
        inner_kernel,
        grid=(STEPS,),
        in_specs=[rows(EG), rows(VG), rows(LANES), rows(LANES), rows(LANES), spec((8, LANES))],
        out_specs=[rows(EG), rows(2 * N)],
        out_shape=[shaped(TOKENS, EG), shaped(TOKENS, 2 * N)],
        compiler_params=SMALL,
        cost_estimate=cost(3 << 30, 9 << 20),
        name="inner",
    )(dy, conv, dt, cum, flags, ids)


def backward(
    place, u, d_bc, dy, y, conv, dt, cum, r, flags, starts, reach, arrived, ends, reach_back, arrivals,
    final, v, wide, taps, head, summer, edge_flags,
):
    def back_state():
        return spec((AT_ONCE, N, EG), lambda c: (STEPS - 1 - c, 0, 0))

    return pl.pallas_call(
        backward_kernel,
        grid=(STEPS,),
        in_specs=[
            pl.BlockSpec(memory_space=pltpu.SMEM),
            rows_back(EG),
            rows_back(2 * N),
            rows_back(EG),
            rows_back(EG),
            rows_back(VG),
            rows_back(LANES),
            rows_back(LANES),
            rows_back(LANES),
            rows_back(LANES),
            back_state(),
            rows_back(EG, 8 * AT_ONCE),
            spec((N, EG)),
            back_state(),
            rows_back(EG, 8 * AT_ONCE),
        ]
        + [spec((STATE_ROWS, EG))] * 4
        + [
            rows_back(EG),
            spec((8, EG), lambda c: (previous(STEPS - 1 - c), 0)),
            spec((8, EG)),
            spec((8, VG)),
            spec((8, LANES)),
            spec((EG, LANES)),
            spec((8, LANES)),
        ],
        out_specs=[
            rows_back(EG),
            spec((EDGE, EG)),
            spec((N, SPAN), lambda c: (0, STEPS - 1 - c)),
            spec((N, SPAN), lambda c: (0, STEPS - 1 - c)),
            rows_back(LANES),
            spec((8, EG)),
            spec((8, LANES)),
        ],
        out_shape=[
            shaped(TOKENS, EG, dtype=BF16),
            shaped(EDGE, EG, dtype=BF16),
            shaped(N, TOKENS),
            shaped(N, TOKENS),
            shaped(TOKENS, LANES),
            shaped(8, EG),
            shaped(8, LANES),
        ],
        scratch_shapes=[
            pltpu.VMEM((8, EG), F32),
            pltpu.VMEM((8, LANES), F32),
            pltpu.VMEM((N, EG), F32),
        ],
        compiler_params=SMALL,
        cost_estimate=cost(3 << 29, 20 << 20),
        name="backward",
    )(
        place, u, d_bc, dy, y, conv, dt, cum, r, flags, starts, reach, arrived, ends, reach_back,
        *arrivals, final, v, v, wide, taps, head, summer, edge_flags,
    )


def shared(team, got, conv, v, dr, dv, d_edge, flags, edge_flags, taps):
    def turned(step):
        return jnp.maximum(STEPS - 1 - step, 0)

    def lanes_of(block):
        return spec((SPAN, LANES), lambda c: (turned(c), block))

    def before(block):
        return spec((8, LANES), lambda c: (previous(turned(c)), block))

    b, c_block = EG // LANES, EG // LANES + 1
    def kernel(team_ref, a, b, c, d, *refs):
        shared_kernel(team_ref, (a, b, c, d), *refs)

    return pl.pallas_call(
        kernel,
        grid=(STEPS + 1,),
        in_specs=[
            pl.BlockSpec(memory_space=pltpu.SMEM),
            *[spec((BG, SPAN), lambda c: (0, turned(c)))] * 4,
            lanes_of(b),
            lanes_of(c_block),
            lanes_of(b),
            lanes_of(c_block),
            before(b),
            before(c_block),
            lanes_of(0),
            spec((SPAN, EG), lambda c: (turned(c), 0)),
            spec((EDGE, EG)),
            lanes_of(0),
            spec((8, LANES)),
            spec((8, LANES)),
        ],
        out_specs=[
            spec((SPAN, LATE_COLS), lambda c: (jnp.where(c == STEPS, STEPS, turned(c)), 0)),
            spec((8, LANES)),
        ],
        out_shape=[shaped(TOKENS + EDGE, LATE_COLS, dtype=BF16), shaped(8, LANES)],
        scratch_shapes=[pltpu.VMEM((8, LANES), F32)],
        compiler_params=SMALL,
        cost_estimate=cost(1 << 27, 6 << 20),
        name="shared",
    )(team, *got, conv, conv, v, v, v, v, dr, dv, d_edge, flags, edge_flags, taps)


def gram(which, x):
    count, n, _ = x.shape
    blocks = len(triangle(n))
    return pl.pallas_call(
        gram_kernel,
        in_specs=[pl.BlockSpec(memory_space=pltpu.SMEM), pl.BlockSpec(memory_space=pl.ANY)],
        out_specs=pl.BlockSpec(memory_space=pl.ANY),
        out_shape=shaped(blocks, TILE, TILE),
        scratch_shapes=[
            pltpu.VMEM((count, n, IN_COLS), BF16),
            pltpu.VMEM((blocks, TILE, TILE), F32),
            pltpu.SemaphoreType.DMA((count,)),
            pltpu.SemaphoreType.DMA((n // TILE,)),
        ],
        compiler_params=LARGE,
        cost_estimate=cost(n * n * count * BLOCK * 3 // 5, 14 << 20),
        name="gram",
    )(which.astype(jnp.int32).reshape(1), x)


def chain(own, got, pick):
    n = pick.shape[1]
    whole = pl.BlockSpec(memory_space=pltpu.VMEM)
    return pl.pallas_call(
        chain_kernel,
        out_shape=jax.ShapeDtypeStruct(pick.shape, F32),
        in_specs=[whole, whole, whole],
        out_specs=whole,
        scratch_shapes=[pltpu.VMEM((n, n), BF16)] * 4
        + [pltpu.VMEM((NS_STEPS - 1, n, n), BF16)],
        compiler_params=pltpu.CompilerParams(vmem_limit_bytes=52 << 20),
        cost_estimate=cost(14 * n * n * n, 11 << 20),
        name="chain",
    )(own, got, pick)


def summaries(packed, direction):
    size = lax.axis_size("x")
    return [
        lax.ppermute(
            packed,
            "x",
            [(s, s + direction * k) for s in range(size) if 0 <= s + direction * k < size],
        )
        for k in range(1, size)
    ]


def blocks_of_columns(in_rows, out_rows):
    count = in_rows.shape[0]
    kind = in_rows.dtype
    z = in_rows[:, :E].reshape(count, G, EG)
    xs = in_rows[:, E : 2 * E].reshape(count, G, EG)
    bc = in_rows[:, 2 * E : 2 * E + 2 * N].reshape(count, G, BG)
    r = in_rows[:, 2 * E + 2 * N :].reshape(count, G, HG)
    fill = jnp.zeros((count, G, LANES - BG - HG), kind)
    out = out_rows.reshape(count, G, EG)
    return jnp.concatenate([z, xs, bc, r, fill, out], axis=2).transpose(1, 0, 2)


def rows_of_blocks(blocks):
    count = blocks.shape[1]
    b = blocks.transpose(1, 0, 2)
    pieces = [
        b[:, :, :EG].reshape(count, E),
        b[:, :, EG : 2 * EG].reshape(count, E),
        b[:, :, 2 * EG : 2 * EG + BG].reshape(count, 2 * N),
        b[:, :, 2 * EG + BG : 2 * EG + BG + HG].reshape(count, H),
    ]
    return jnp.concatenate(pieces, axis=1), b[:, :, IN_COLS:].reshape(count, E)


def along_y(own):
    size = lax.axis_size("y")
    return [own] + [
        lax.ppermute(own, "y", [(s, (s + k) % size) for s in range(size)]) for k in range(1, size)
    ]


def team_sum(values):
    values = values + lax.ppermute(values, "c", [(0, 1), (1, 0)])
    return sum(along_y(values))


def after(value, *others):
    return lax.optimization_barrier((value,) + others)[0]


def local(
    hidden,
    segments,
    norm_gain,
    in_weight,
    conv_weight,
    conv_bias,
    dt_bias,
    a_log,
    skip_scale,
    gate_gain,
    out_weight,
    cotangent,
    in_momentum,
    out_momentum,
    vector_momentum,
):
    zi, xi, yi, ci = (lax.axis_index(a) for a in EVERY)
    team = yi * 2 + ci
    count = in_weight.shape[0]
    team_count = G * count
    swap = [(0, 1), (1, 0)]
    first = ci == 0

    def mine(values, width, start=0, axis=-1):
        return lax.dynamic_slice_in_dim(values, start + team * width, width, axis % values.ndim)

    z_w = in_weight[:, :E].reshape(count, G, EG)
    xs_w = in_weight[:, E : 2 * E].reshape(count, G, EG)
    bc_w = jnp.broadcast_to(in_weight[:, None, 2 * E : 2 * E + 2 * N], (count, G, 2 * N))
    r_w = jnp.pad(
        in_weight[:, 2 * E + 2 * N :].reshape(count, G, HG), ((0, 0), (0, 0), (0, LANES - HG))
    )
    out_w = out_weight.reshape(count, G, EG)
    sent = jnp.concatenate([z_w, xs_w, bc_w, r_w, out_w], axis=2).transpose(1, 0, 2)
    got = lax.all_to_all(sent, TEAM, 0, 0, tiled=True).reshape(team_count, -1)
    weights = lax.all_gather(got, ROWS, axis=0, tiled=True)

    numbers = jnp.pad(segments.astype(BF16)[:, None], ((0, 0), (0, LANES - 1)))
    pieces = along_y(jnp.concatenate([hidden, numbers], axis=1))
    momentum_block = lax.all_to_all(
        blocks_of_columns(
            *(after(m, got).astype(BF16) for m in (in_momentum, out_momentum))
        ),
        TEAM,
        0,
        0,
        tiled=True,
    ).reshape(team_count, BLOCK)
    conv_all = jnp.concatenate([conv_weight, conv_bias[None, :]], axis=0)
    taps = jnp.pad(
        jnp.concatenate([mine(conv_all[:, :E], EG), conv_all[:, E:]], axis=1),
        ((0, 8 - TAPS - 1), (0, 0)),
    )
    taps_shared = jnp.pad(mine(conv_all[:, E:], BG), ((0, 8 - TAPS - 1), (0, LANES - BG)))
    head = jnp.pad(
        jnp.stack([mine(dt_bias, HG), jnp.exp(mine(a_log, HG))]), ((0, 6), (0, LANES - HG))
    )
    wide = jnp.pad(
        jnp.stack([jnp.repeat(mine(skip_scale, HG), HEAD), mine(gate_gain, EG)]), ((0, 6), (0, 0))
    )
    summer = (
        lax.broadcasted_iota(jnp.int32, (EG, LANES), 0) // HEAD
        == lax.broadcasted_iota(jnp.int32, (EG, LANES), 1)
    ).astype(BF16)
    pieces, momentum_block, taps, taps_shared, head, wide, summer = lax.optimization_barrier(
        (pieces, momentum_block, taps, taps_shared, head, wide, summer)
    )
    own_rows = jnp.stack(pieces)
    other_rows = lax.ppermute(own_rows, "c", swap)
    q_pieces = along_y(after(cotangent, own_rows))
    place = jnp.stack([yi, ci]).astype(jnp.int32)
    size_x, size_y = lax.axis_size("x"), lax.axis_size("y")
    end_rows = lax.dynamic_index_in_dim(
        jnp.where(first, other_rows[:, CHUNK - EDGE :], own_rows[:, CHUNK - EDGE :]),
        (yi + 1) % size_y,
        0,
        False,
    )
    edge_rows_in = lax.ppermute(end_rows, "x", [(s, s + 1) for s in range(size_x - 1)])
    by_distance = jnp.stack([own_rows[:, :, D], other_rows[:, :, D]]).astype(F32)
    by_core = jnp.where(first, by_distance, by_distance[::-1])
    team_ids = by_core[:, (yi - jnp.arange(size_y)) % size_y].transpose(1, 0, 2).reshape(-1)
    next_ids = lax.ppermute(team_ids[:LANES], "x", [(s, s - 1) for s in range(1, size_x)])
    ids = jnp.concatenate(
        [
            jnp.where(xi == 0, -1.0, edge_rows_in[EDGE - 8 :, D].astype(F32)),
            team_ids,
            jnp.where(xi == size_x - 1, -1.0, next_ids[:8]),
        ]
    )

    def flag_lanes(at, size):
        own = ids[at : at + size]
        same = [(ids[at - k : at - k + size] == own).astype(F32) for k in range(TAPS)]
        ahead = [(ids[at + k : at + k + size] == own).astype(F32) for k in range(TAPS)]
        return own, same + ahead

    own_ids, lanes = flag_lanes(8, TOKENS)
    by_piece = own_ids.reshape(PIECES, CHUNK)
    before = ids[7 : 7 + TOKENS].reshape(PIECES, CHUNK)[:, :1]
    last = by_piece[:, CHUNK - 1 :]
    lanes = lanes + [
        jnp.zeros((TOKENS,), F32),
        (by_piece == before).astype(F32).reshape(-1),
        (by_piece == last).astype(F32).reshape(-1),
        jnp.broadcast_to((last == before).astype(F32), (PIECES, CHUNK)).reshape(-1),
        own_ids,
    ]
    flags = jnp.pad(jnp.stack(lanes, axis=1), ((0, 0), (0, LANES - len(lanes))))
    edge_ids = jnp.pad(ids, (8, 0), constant_values=-1.0)[: 8 + 16]
    edge_own = edge_ids[8:16]
    edge_flags = jnp.pad(
        jnp.stack(
            [jnp.zeros((8,), F32)] * AHEAD
            + [(edge_ids[8 + k : 16 + k] == edge_own).astype(F32) for k in range(TAPS)],
            axis=1,
        ),
        ((0, 0), (0, LANES - AHEAD - TAPS)),
    )

    q_pieces, flags, edge_flags = lax.optimization_barrier((q_pieces, flags, edge_flags))
    q_own = jnp.stack(q_pieces)
    q_other = lax.ppermute(q_own, "c", swap)

    normed, z, v, r = project(
        place, own_rows, other_rows, edge_rows_in, weights, norm_gain[None, :]
    )
    conv, dt, cum, y_part, starts, reach, gain, packed = forward(v, r, flags, by_piece, taps, head)
    arrivals = summaries(packed, 1)
    q_team, d_gated = incoming(place, q_own, q_other, weights)
    y, sums, arrived = outputs(y_part, conv, cum, flags, z, d_gated, reach, arrivals, wide)
    sums = team_sum(sums)
    gated, dz, dy, ends, reach_back, d_gate, packed_back = gate(
        y, z, d_gated, conv, cum, flags, gain, sums, wide
    )
    early = early_products(normed, q_team, dz, gated)
    dy, packed_back, early = lax.optimization_barrier((dy, packed_back, early))
    early_sum = lax.psum_scatter(early, ROWS, scatter_dimension=0, tiled=True).astype(F32)
    arrivals_back = summaries(packed_back, -1)

    u, d_bc = inner(dy, conv, dt, cum, flags, by_piece)
    dv, d_edge, kept, sent_bc, dr, wide_sums, head_sums_out = backward(
        place, u, d_bc, dy, y, conv, dt, cum, r, flags, starts, reach, arrived, ends, reach_back,
        arrivals_back, packed, v, wide, taps, head, summer, edge_flags,
    )
    summed = (kept + lax.ppermute(sent_bc, "c", swap)).reshape(size_y, BG, TOKENS)

    def piece_for(k):
        return lax.dynamic_index_in_dim(summed, (yi + k) % size_y, 0, False)

    d_bc_got = [piece_for(0)] + [
        lax.ppermute(piece_for(k), "y", [(s, (s + k) % size_y) for s in range(size_y)])
        for k in range(1, size_y)
    ]
    late, shared_sums = shared(
        team.reshape(1), d_bc_got, conv, v, dr, dv, d_edge, flags, edge_flags, taps_shared
    )
    late_partial = dot(normed, late, TN).astype(BF16)
    late_parts = lax.all_to_all(
        late_partial.reshape(16, team_count, LATE_COLS), ROWS, 0, 0, tiled=True
    )
    late_sum = jnp.sum(late_parts.astype(F32), axis=0)

    sums_block = jnp.concatenate([early_sum[:, :EG], late_sum, early_sum[:, EG:]], axis=1)
    momenta = MATRIX_MOMENTUM * momentum_block.astype(F32) + sums_block
    x_all = lax.all_gather(momenta.astype(BF16), ("y", "z", "x")).reshape(4, D, BLOCK)

    late_back = lax.ppermute(
        late[TOKENS:], "x", [(s, s - 1) for s in range(1, lax.axis_size("x"))]
    )
    late, late_back, dz, gated, late_sum = lax.optimization_barrier(
        (late, late_back, dz, gated, late_sum)
    )
    d_projected = jnp.concatenate(
        [
            dz,
            jnp.concatenate(
                [late[: TOKENS - EDGE], late[TOKENS - EDGE : TOKENS] + late_back], axis=0
            ),
        ],
        axis=1,
    )
    w_own = jnp.concatenate(
        [
            weights[:, : 2 * EG],
            mine(weights[:, 2 * EG : 2 * EG + 2 * N], BG),
            weights[:, 2 * EG + 2 * N : 2 * EG + 2 * N + HG],
            jnp.zeros((D, LANES - BG - HG), BF16),
        ],
        axis=1,
    )
    d_normed_part = dot(d_projected, w_own, NT)
    d_norm_gain = jnp.sum(d_normed_part * normed[:TOKENS].astype(F32), axis=0) / norm_gain
    mixed_part = dot(gated, weights[:, FORWARD_COLS:], NT)

    vector = jnp.concatenate(
        [
            d_norm_gain,
            jnp.concatenate(
                [wide_sums[: TAPS + 1], shared_sums[: TAPS + 1, :BG]], axis=1
            ).reshape(-1),
            d_gate[0],
            head_sums_out[:3, :HG].reshape(-1),
        ]
    )
    vector = jnp.pad(vector, (0, -vector.shape[0] % 1024)).reshape(-1, LANES)
    vector = jnp.sum(lax.all_gather(vector, ROWS), axis=0)
    vector = lax.all_gather(vector, TEAM).reshape(G, -1)
    own = EG + BG
    grad_gain = jnp.sum(vector[:, :D], axis=0)
    conv_parts = vector[:, D : D + (TAPS + 1) * own].reshape(G, TAPS + 1, own).transpose(1, 0, 2)
    conv_parts = jnp.concatenate(
        [
            conv_parts[:, :, :EG].reshape(TAPS + 1, E),
            conv_parts[:, :, EG:].reshape(TAPS + 1, 2 * N),
        ],
        axis=1,
    )
    rest = vector[:, D + (TAPS + 1) * own :]
    heads = rest[:, EG : EG + 3 * HG].reshape(G, 3, HG).transpose(1, 0, 2).reshape(-1)
    vector_grad = jnp.concatenate(
        [grad_gain, conv_parts.reshape(-1), heads, rest[:, :EG].reshape(-1)]
    )
    vector_old = jnp.concatenate(
        [norm_gain, conv_weight.reshape(-1), conv_bias, dt_bias, a_log, skip_scale, gate_gain]
    )
    vector_momentum_new = VECTOR_MOMENTUM * vector_momentum + (1.0 - VECTOR_MOMENTUM) * vector_grad
    vector_new = vector_old - VECTOR_RATE * vector_momentum_new
    grad_rows = lax.all_to_all(
        sums_block.reshape(G, count, BLOCK), TEAM, 0, 0, tiled=True
    )
    in_grad, out_grad = rows_of_blocks(grad_rows)
    in_momentum_new = MATRIX_MOMENTUM * in_momentum + in_grad
    out_momentum_new = MATRIX_MOMENTUM * out_momentum + out_grad

    x_all, d_normed_part, mixed_part, vector_grad, in_grad = lax.optimization_barrier(
        (x_all, d_normed_part, mixed_part, vector_grad, in_grad)
    )
    gram_sent = gram(ci == 1, x_all)
    gram_got = lax.ppermute(gram_sent, "c", swap)
    gram_own = gram(after(first, gram_sent), x_all)
    chip_row = (zi * 4 + xi) * team_count + yi * (2 * count)
    pick = (
        lax.broadcasted_iota(jnp.int32, (2 * count, D), 1)
        == lax.broadcasted_iota(jnp.int32, (2 * count, D), 0) + chip_row
    ).astype(F32)
    t_own = chain(gram_own, gram_got, pick)
    d_normed = lax.psum_scatter(d_normed_part, TEAM, scatter_dimension=0, tiled=True)
    mixed = lax.psum_scatter(mixed_part, TEAM, scatter_dimension=0, tiled=True)
    hidden_own = hidden.astype(F32)
    block_output = (hidden_own + mixed).astype(BF16)
    scale_own = lax.rsqrt(jnp.mean(hidden_own * hidden_own, axis=-1, keepdims=True) + EPSILON)
    unit_own = hidden_own * scale_own
    d_unit = d_normed * norm_gain
    d_hidden = scale_own * (
        d_unit - unit_own * jnp.mean(d_unit * unit_own, axis=-1, keepdims=True)
    )
    input_grad = cotangent.astype(F32) + d_hidden

    t_other = lax.ppermute(t_own, "c", swap)
    t_in = jnp.where(first, t_own, t_other)
    t_out = jnp.where(first, t_other, t_own)

    def applied(t, x):
        both = jnp.einsum(
            "rk,ykn->yrn", jnp.concatenate(parts(t), axis=0), x, preferred_element_type=F32
        )
        return both[:, : 2 * count] + both[:, 2 * count :]

    halves = jnp.concatenate(
        [applied(t_in, x_all[:, :, :IN_COLS]), applied(t_out, x_all[:, :, IN_COLS:])], axis=2
    )
    half_own = lax.dynamic_slice_in_dim(halves, ci * count, count, 1)
    half_sent = lax.dynamic_slice_in_dim(halves, (1 - ci) * count, count, 1)
    half_got = lax.ppermute(half_sent, "c", swap)
    both = jnp.stack(
        [jnp.where(first, half_own, half_got), jnp.where(first, half_got, half_own)], axis=1
    ).reshape(G, count, BLOCK)
    step_in, step_out = rows_of_blocks(both)
    in_weight_new = in_weight.astype(F32) - MATRIX_RATE * math.sqrt(PROJ / D) * step_in
    out_weight_new = out_weight.astype(F32) - MATRIX_RATE * math.sqrt(E / D) * step_out
    return (
        block_output,
        input_grad,
        in_grad,
        in_momentum_new,
        in_weight_new,
        out_grad,
        out_momentum_new,
        out_weight_new,
        vector_grad,
        vector_momentum_new,
        vector_new,
    )


def solution(mesh):
    grid = Mesh(mesh.devices.reshape(4, 4, 4, 2), EVERY)
    split = P(EVERY, None)
    return jax.shard_map(
        local,
        mesh=grid,
        in_specs=(
            split,
            P(EVERY),
            P(),
            split,
            P(),
            P(),
            P(),
            P(),
            P(),
            P(),
            split,
            split,
            split,
            split,
            P(),
        ),
        out_specs=(split,) * 8 + (P(),) * 3,
        check_vma=False,
    )
```

profile of v0, /device:TPU:1, one launch (start us, length us, event | category | flops | bytes accessed | tf_op | source)
XLA Modules:
  0.0 458.1 jit_solution(2624388677777459524)
XLA Ops:
  11.1 13.9 %all_to_all.20 = bf16[8,12,1536]{2,1,0:T(8,128)(2,1)S(1)} all-to-all(bf16[8,12,1536]{2,1,0:T(8,128)(2,1)S(1)} %bitcast.156), channel_id=1, replica_groups=mesh['z'=4,'x'=4,'y'=4,'c'=2] {'y','c'}, dimensions={0} | all-to-all | bytes 589824 | tf_op jit(solution)/shard_map/all_to_all | solution.py:1206
  30.8 6.4 %all-to-all-start.1 = ((bf16[8,12,1280]{2,1,0:T(8,128)(2,1)}), bf16[8,12,1280]{2,1,0:T(8,128)(2,1)S(1)}, u32[]{:S(2)}, u32[]{:S(2)}) async-start(bf16[8,12,1280]{2,1,0:T(8,128)(2,1)} %bitcast.2), calls=%async_computation.1 | async-start | bytes 655360 | tf_op jit(solution)/shard_map/all_to_all | solution.py:1211
  37.4 14.8 %all-to-all-done.1 = bf16[8,12,1280]{2,1,0:T(8,128)(2,1)S(1)} async-done(((bf16[8,12,1280]{2,1,0:T(8,128)(2,1)}), bf16[8,12,1280]{2,1,0:T(8,128)(2,1)S(1)}, u32[]{:S(2)}, u32[]{:S(2)}) %all-to-all-start.1) | async-done | bytes 245792 | tf_op jit(solution)/shard_map/all_to_all | solution.py:1211
  71.7 6.3 %collective-permute-done.5 = bf16[128,1536]{1,0:T(8,128)(2,1)} collective-permute-done((bf16[128,1536]{1,0:T(8,128)(2,1)S(1)}, bf16[128,1536]{1,0:T(8,128)(2,1)}, u32[]{:S(2)}, u32[]{:S(2)}) %collective-permute-start.5) | collective-permute-done | bytes 393248 | tf_op jit(solution)/shard_map/ppermute | solution.py:1158
  85.4 9.5 %project.1 = (bf16[1040,1536]{1,0:T(8,128)(2,1)S(1)}, f32[1040,384]{1,0:T(8,128)S(1)}, f32[1040,640]{1,0:T(8,128)S(1)}, f32[1040,128]{1,0:T(8,128)S(1)}) custom-call(s32[2]{0:T(128)S(1)} %pad_add_fusion.core_ref, bf16[4,128,1664]{2,1,0:T(8,128)(2,1)S(1)} %copy-done.16, bf16[4,128,1664]{2,1,0:T(8,128)(2,1)} %collective-permute-done.3.other_ref, ...), custom_call_target="tpu_custom_call" | custom-call | flops 3680501760 | bytes 16777216 | tf_op jit(solution)/shard_map/project/pallas_call | solution.py:802
  95.0 8.6 %forward.1 = (f32[1024,640]{1,0:T(8,128)S(1)}, f32[1024,128]{1,0:T(8,128)S(1)}, f32[1024,128]{1,0:T(8,128)S(1)}, f32[1024,384]{1,0:T(8,128)S(1)}, f32[8,128,384]...) custom-call(f32[1040,640]{1,0:T(8,128)S(1)} %get-tuple-element.85.v_ref.before_ref.refs_2_, ...), custom_call_target="tpu_custom_call" | custom-call | flops 3221225472 | bytes 14680064 | tf_op jit(solution)/shard_map/forward/pallas_call | solution.py:872
  104.5 4.4 collective-permute-start.12
  112.7 4.7 %incoming.1 = (bf16[1024,1536]{1,0:T(8,128)(2,1)S(1)}, f32[1024,384]{1,0:T(8,128)S(1)}) custom-call(s32[2]{0:T(128)S(1)} %pad_add_fusion.core_ref, bf16[4,128,1536]{2,1,0:T(8,128)(2,1)} %pad_maximum_fusion.1.own_ref, bf16[4,128,1536]{2,1,0:T(8,128)(2,1)} %collective-permute-done.9.other_ref, bf16[1536,1536]{1,0:T(8,128)(2,1)S(1)} %bitcast.121), custom_call_target="tpu_custom_call" | custom-call | flops 1207959552 | bytes 9437184 | tf_op jit(solution)/shard_map/incoming/pallas_call | solution.py:834
  129.4 4.1 gate.1
  137.2 5.1 %early.1 = bf16[1536,768]{1,0:T(8,128)(2,1)S(1)} custom-call(bf16[1040,1536]{1,0:T(8,128)(2,1)S(1)} %get-tuple-element.108.normed_ref, bf16[1024,1536]{1,0:T(8,128)(2,1)S(1)} %get-tuple-element.109.q_ref, bf16[1024,384]{1,0:T(8,128)(2,1)S(1)} %get-tuple-element.131.dz_ref, bf16[1024,384]{1,0:T(8,128)(2,1)S(1)} %get-tuple-element.134.gated_ref), custom_call_target="tpu_custom_call" | custom-call | flops 2415919104 | bytes 13631488 | tf_op jit(solution)/shard_map/early/pallas_call | solution.py:854
  154.8 5.8 %inner.1 = (f32[1024,384]{1,0:T(8,128)S(1)}, f32[1024,256]{1,0:T(8,128)S(1)}) custom-call(f32[1024,384]{1,0:T(8,128)S(1)} %copy-done.20, f32[1024,640]{1,0:T(8,128)S(1)} %copy-done.1, f32[1024,128]{1,0:T(8,128)S(1)} %copy-done.32, f32[1024,128]{1,0:T(8,128)S(1)} %copy-done.9, f32[1024,128]{1,0:T(8,128)S(1)} %pad.44.flags_ref.refs_9_, f32[8,128]{1,0:T(8,128)S(1)} %bitcast.130), custom_call_target="tpu_custom_call" | custom-call | flops 3221225472 | bytes 9437184 | tf_op jit(solution)/shard_map/inner/pallas_call | solution.py:957
  160.7 11.1 %backward.1 = (bf16[1024,384]{1,0:T(8,128)(2,1)S(1)}, bf16[16,384]{1,0:T(8,128)(2,1)S(1)}, f32[128,1024]{1,0:T(8,128)S(1)}, f32[128,1024]{1,0:T(8,128)}, f32[102...) custom-call(s32[2]{0:T(128)S(1)} %copy-done.41, f32[1024,384]{1,0:T(8,128)S(1)} %get-tuple-element.115.u_ref, ...), custom_call_target="tpu_custom_call" | custom-call | flops 1610612736 | bytes 20971520 | tf_op jit(solution)/shard_map/backward/pallas_call | solution.py:976
  197.4 34.0 %all_to_all.21 = bf16[16,96,512]{2,1,0:T(8,128)(2,1)S(1)} all-to-all(bf16[16,96,512]{2,1,0:T(8,128)(2,1)S(1)} %bitcast.141), channel_id=1, replica_groups=mesh['z'=4,'x'=4,'y'=4,'c'=2] {'z','x'}, dimensions={0} | all-to-all | bytes 3145728 | tf_op jit(solution)/shard_map/all_to_all | solution.py:1330
  245.5 8.4 %multiply_reduce_fusion = (f32[1536]{0:T(1024)S(1)}, f32[1024,1536]{1,0:T(8,128)}) fusion(bf16[1040,1536]{1,0:T(8,128)(2,1)} %copy-done.13, bf16[1536,6]{1,0:T(8,128)(2,1)S(1)} %slice-done.2, bf16[1536,32]{1,0:T(8,128)(2,1)} %constant_dynamic-slice_fusion, bf16[1536,768]{1,0:T(8,128)(2,1)S(1)} %slice-done.4, bf16[896]{0:T(1024)(128)(2,1)} %pad.66.clone, ...), kind=kOutput, calls=%fused_computation.3 | convolution fusion | flops 2839804416 | bytes 13756160 | tf_op jit(solution)/shard_map/dot_general | solution.py:58
  254.8 17.3 %all_gather.21 = f32[16,32,128]{2,1,0:T(8,128)S(1)} all-gather(f32[1,32,128]{2,1,0:T(8,128)S(1)} %pad_bitcast_fusion), channel_id=1, replica_groups=mesh['z'=4,'x'=4,'y'=4,'c'=2] {'z','x'}, dimensions={0}, use_global_device_ids=true | all-gather | bytes 278528 | tf_op jit(solution)/shard_map/all_gather | solution.py:1378
  272.2 20.1 %all-gather.1 = f32[256,128]{1,0:T(8,128)S(1)} all-gather(f32[32,128]{1,0:T(8,128)S(1)} %reduce_sum.56), channel_id=3, replica_groups=mesh['z'=4,'x'=4,'y'=4,'c'=2] {'y','c'}, dimensions={0}, use_global_device_ids=true | all-gather | bytes 147456 | tf_op jit(solution)/shard_map/all_gather | solution.py:1379
  297.5 5.8 %fusion.20 = f32[1024,1536]{1,0:T(8,128)} fusion(bf16[1024,384]{1,0:T(8,128)(2,1)S(1)} %copy-done.12, bf16[1536,1536]{1,0:T(8,128)(2,1)} %all-gather.5.cloned.1.call-done.w_ref), kind=kOutput, calls=%fused_computation.27 | convolution fusion | flops 1207959552 | bytes 8257536 | tf_op jit(solution)/shard_map/dot_general | solution.py:58
  303.3 12.4 %all-to-all-done.3 = f32[8,12,1280]{2,1,0:T(8,128)S(1)} async-done(((f32[8,12,1280]{2,1,0:T(8,128)}), f32[8,12,1280]{2,1,0:T(8,128)S(1)}, u32[]{:S(2)}, u32[]{:S(2)}) %all-to-all-start.3) | async-done | bytes 491552 | tf_op jit(solution)/shard_map/all_to_all | solution.py:1400
  316.4 24.6 %all-gather.7.cloned.1.call-done = bf16[6144,1280]{1,0:T(8,128)(2,1)} async-done(((bf16[96,1280]{1,0:T(8,128)(2,1)}), bf16[6144,1280]{1,0:T(8,128)(2,1)}) %all-gather.7.cloned.1.call-update) | async-done | bytes 15728656 | tf_op jit(solution)/shard_map/all_gather | solution.py:1337
  341.2 14.6 %gram.2 = f32[21,256,256]{2,1,0:T(8,128)} custom-call(s32[1]{0:T(128)} %bitcast.46.which_ref, bf16[4,1536,1280]{2,1,0:T(8,128)(2,1)} %bitcast.185), custom_call_target="tpu_custom_call" | custom-call | flops 7247757312 | bytes 14680064 | tf_op jit(solution)/shard_map/gram/pallas_call | solution.py:1086
  357.1 7.8 %gram.3.own_ref = f32[21,256,256]{2,1,0:T(8,128)} custom-call(s32[1]{0:T(128)} %bitcast.47.which_ref, bf16[4,1536,1280]{2,1,0:T(8,128)(2,1)} %bitcast.186), custom_call_target="tpu_custom_call" | custom-call | flops 7247757312 | bytes 14680064 | tf_op jit(solution)/shard_map/gram/pallas_call | solution.py:1086
  365.8 60.5 %chain.1 = f32[24,1536]{1,0:T(8,128)S(1)} custom-call(f32[21,256,256]{2,1,0:T(8,128)} %gram.3.own_ref, f32[21,256,256]{2,1,0:T(8,128)} %collective-permute-done.25.got_ref, f32[24,1536]{1,0:T(8,128)S(1)} %fusion.43.pick_ref), custom_call_target="tpu_custom_call" | custom-call | flops 50734301184 | bytes 11534336 | tf_op jit(solution)/shard_map/chain/pallas_call | solution.py:1106
  426.4 6.4 %collective-permute-start.26 = (f32[24,1536]{1,0:T(8,128)S(1)}, f32[24,1536]{1,0:T(8,128)S(1)}, u32[]{:S(2)}, u32[]{:S(2)}) collective-permute-start(f32[24,1536]{1,0:T(8,128)S(1)} %chain.1), channel_id=1, source_target_pairs={{0,1},{1,0},{2,3},{3,2},{4,5},{5,4},{6,7},{7,6},{8,9},{9,8},{10,11... | collective-permute-start | bytes 442376 | tf_op jit(solution)/shard_map/ppermute | solution.py:1431
  437.1 5.3 %fusion.17 = f32[4,48,896]{2,1,0:T(8,128)S(1)} fusion(bf16[4,1536,1280]{2,1,0:T(8,128)(2,1)} %bitcast.188, bf16[24,1536]{1,0:T(8,128)(2,1)S(1)} %get-tuple-element.171, bf16[24,1536]{1,0:T(8,128)(2,1)S(1)} %get-tuple-element.169), kind=kOutput, calls=%fused_computation.23 | convolution fusion | flops 528777216 | bytes 11845632 | tf_op jit(solution)/shard_map/rk,ykn->yrn/dot_general | solution.py:1436
  (437 shorter events, 130.4 us)
Async XLA Ops:
  7.3 74.4 %all-gather.5.cloned.1.call-start = ((), (), s32[]{:S(2)}) async-start(), calls=%async_computation.7 | async-start | bytes 5013504 | tf_op jit(solution)/shard_map/all_gather | solution.py:1207
  25.9 27.0 %collective-permute-start.2 = (bf16[128,1664]{1,0:T(8,128)(2,1)S(1)}, bf16[128,1664]{1,0:T(8,128)(2,1)S(1)}, u32[]{:S(2)}, u32[]{:S(2)}) collective-permute-start(bf16[128,1664]{1,0:T(8,128)(2,1)S(1)} %fusion.34), channel_id=1, source_target_pairs={{0,6},{2,0},{4,2},{6,4},{1,7},{3,1},{5,3},{7,5},{8,14},{10,8},{12,... | collective-permute-start | bytes 1277960 | tf_op jit(solution)/shard_map/ppermute | solution.py:1158
  26.9 26.1 %collective-permute-start.1 = (bf16[128,1664]{1,0:T(8,128)(2,1)S(1)}, bf16[128,1664]{1,0:T(8,128)(2,1)S(1)}, u32[]{:S(2)}, u32[]{:S(2)}) collective-permute-start(bf16[128,1664]{1,0:T(8,128)(2,1)S(1)} %fusion.34), channel_id=1, source_target_pairs={{0,4},{2,6},{4,0},{6,2},{1,5},{3,7},{5,1},{7,3},{8,12},{10,14},{12... | collective-permute-start | bytes 1277960 | tf_op jit(solution)/shard_map/ppermute | solution.py:1158
  28.1 24.9 %collective-permute-start = (bf16[128,1664]{1,0:T(8,128)(2,1)S(1)}, bf16[128,1664]{1,0:T(8,128)(2,1)S(1)}, u32[]{:S(2)}, u32[]{:S(2)}) collective-permute-start(bf16[128,1664]{1,0:T(8,128)(2,1)S(1)} %fusion.34), channel_id=1, source_target_pairs={{0,2},{2,4},{4,6},{6,0},{1,3},{3,5},{5,7},{7,1},{8,10},{10,12},{12... | collective-permute-start | bytes 1277960 | tf_op jit(solution)/shard_map/ppermute | solution.py:1158
  30.8 21.4 %all-to-all-start.1 = ((bf16[8,12,1280]{2,1,0:T(8,128)(2,1)}), bf16[8,12,1280]{2,1,0:T(8,128)(2,1)S(1)}, u32[]{:S(2)}, u32[]{:S(2)}) async-start(bf16[8,12,1280]{2,1,0:T(8,128)(2,1)} %bitcast.2), calls=%async_computation.1 | async-start | bytes 655360 | tf_op jit(solution)/shard_map/all_to_all | solution.py:1211
  37.1 194.5 %reduce-scatter.4.cloned.1.call-start = ((), (), s32[]{:S(2)}) async-start(), calls=%async_computation.8 | async-start | bytes 2506752 | tf_op jit(solution)/shard_map/reduce_scatter | solution.py:1309
  56.8 15.0 %collective-permute-start.7 = (bf16[128,1536]{1,0:T(8,128)(2,1)S(1)}, bf16[128,1536]{1,0:T(8,128)(2,1)}, u32[]{:S(2)}, u32[]{:S(2)}) collective-permute-start(bf16[128,1536]{1,0:T(8,128)(2,1)S(1)} %copy-done.51), channel_id=1, source_target_pairs={{0,6},{2,0},{4,2},{6,4},{1,7},{3,1},{5,3},{7,5},{8,14},{10,8},{12,... | collective-permute-start | bytes 1179656 | tf_op jit(solution)/shard_map/ppermute | solution.py:1158
  56.8 14.9 %collective-permute-start.6 = (bf16[128,1536]{1,0:T(8,128)(2,1)S(1)}, bf16[128,1536]{1,0:T(8,128)(2,1)}, u32[]{:S(2)}, u32[]{:S(2)}) collective-permute-start(bf16[128,1536]{1,0:T(8,128)(2,1)S(1)} %copy-done.51), channel_id=1, source_target_pairs={{0,4},{2,6},{4,0},{6,2},{1,5},{3,7},{5,1},{7,3},{8,12},{10,14},{12... | collective-permute-start | bytes 1179656 | tf_op jit(solution)/shard_map/ppermute | solution.py:1158
  58.1 19.9 %collective-permute-start.5 = (bf16[128,1536]{1,0:T(8,128)(2,1)S(1)}, bf16[128,1536]{1,0:T(8,128)(2,1)}, u32[]{:S(2)}, u32[]{:S(2)}) collective-permute-start(bf16[128,1536]{1,0:T(8,128)(2,1)S(1)} %copy-done.51), channel_id=1, source_target_pairs={{0,2},{2,4},{4,6},{6,0},{1,3},{3,5},{5,7},{7,1},{8,10},{10,12},{12... | collective-permute-start | bytes 1179656 | tf_op jit(solution)/shard_map/ppermute | solution.py:1158
  61.7 6.3 %collective-permute-start.8 = (f32[128]{0:T(128)S(1)}, f32[128]{0:T(128)S(1)}, u32[]{:S(2)}, u32[]{:S(2)}) collective-permute-start(f32[128]{0:T(128)S(1)} %slice.235), channel_id=1, source_target_pairs={{8,0},{16,8},{24,16},{9,1},{17,9},{25,17},{10,2},{18,10},{26,18},{... | collective-permute-start | bytes 1544 | tf_op jit(solution)/shard_map/ppermute | solution.py:1254
  80.6 32.0 %collective-permute-start.9 = (bf16[4,128,1536]{2,1,0:T(8,128)(2,1)}, bf16[4,128,1536]{2,1,0:T(8,128)(2,1)}, u32[]{:S(2)}, u32[]{:S(2)}) collective-permute-start(bf16[4,128,1536]{2,1,0:T(8,128)(2,1)} %pad_maximum_fusion.1.own_ref), channel_id=1, source_target_pairs={{0,1},{1,0},{2,3},{3,2},{4,5},{5,4},{6,7},{7,6},{8,9},{9,8},{10,11... | collective-permute-start | bytes 4718600 | tf_op jit(solution)/shard_map/ppermute | solution.py:1294
  104.5 13.4 %collective-permute-start.12 = (f32[136,384]{1,0:T(8,128)S(1)}, f32[136,384]{1,0:T(8,128)S(1)}, u32[]{:S(2)}, u32[]{:S(2)}) collective-permute-start(f32[136,384]{1,0:T(8,128)S(1)} %get-tuple-element.101.final_ref), channel_id=1, source_target_pairs={{0,24},{1,25},{2,26},{3,27},{4,28},{5,29},{6,30},{7,31},{32,56},{3... | collective-permute-start | bytes 626696 | tf_op jit(solution)/shard_map/ppermute | solution.py:1122
  108.9 9.0 %collective-permute-start.11 = (f32[136,384]{1,0:T(8,128)S(1)}, f32[136,384]{1,0:T(8,128)S(1)}, u32[]{:S(2)}, u32[]{:S(2)}) collective-permute-start(f32[136,384]{1,0:T(8,128)S(1)} %get-tuple-element.101.final_ref), channel_id=1, source_target_pairs={{0,16},{8,24},{1,17},{9,25},{2,18},{10,26},{3,19},{11,27},{4,20},{... | collective-permute-start | bytes 626696 | tf_op jit(solution)/shard_map/ppermute | solution.py:1122
  110.2 9.0 %collective-permute-start.10 = (f32[136,384]{1,0:T(8,128)S(1)}, f32[136,384]{1,0:T(8,128)S(1)}, u32[]{:S(2)}, u32[]{:S(2)}) collective-permute-start(f32[136,384]{1,0:T(8,128)S(1)} %get-tuple-element.101.final_ref), channel_id=1, source_target_pairs={{0,8},{8,16},{16,24},{1,9},{9,17},{17,25},{2,10},{10,18},{18,26},{... | collective-permute-start | bytes 626696 | tf_op jit(solution)/shard_map/ppermute | solution.py:1122
  145.5 195.5 %all-gather.7.cloned.1.call-start = ((), (), s32[]{:S(2)}) async-start(), calls=%async_computation.11 | async-start | bytes 15974400 | tf_op jit(solution)/shard_map/all_gather | solution.py:1337
  145.6 15.0 %collective-permute-start.19 = (f32[136,384]{1,0:T(8,128)}, f32[136,384]{1,0:T(8,128)S(1)}, u32[]{:S(2)}, u32[]{:S(2)}) collective-permute-start(f32[136,384]{1,0:T(8,128)} %copy-done.45), channel_id=1, source_target_pairs={{24,0},{25,1},{26,2},{27,3},{28,4},{29,5},{30,6},{31,7},{56,32},{5... | collective-permute-start | bytes 626696 | tf_op jit(solution)/shard_map/ppermute | solution.py:1122
  146.9 13.7 %collective-permute-start.18 = (f32[136,384]{1,0:T(8,128)}, f32[136,384]{1,0:T(8,128)S(1)}, u32[]{:S(2)}, u32[]{:S(2)}) collective-permute-start(f32[136,384]{1,0:T(8,128)} %copy-done.45), channel_id=1, source_target_pairs={{16,0},{24,8},{17,1},{25,9},{18,2},{26,10},{19,3},{27,11},{20,4},{... | collective-permute-start | bytes 626696 | tf_op jit(solution)/shard_map/ppermute | solution.py:1122
  148.2 12.4 %collective-permute-start.17 = (f32[136,384]{1,0:T(8,128)}, f32[136,384]{1,0:T(8,128)S(1)}, u32[]{:S(2)}, u32[]{:S(2)}) collective-permute-start(f32[136,384]{1,0:T(8,128)} %copy-done.45), channel_id=1, source_target_pairs={{8,0},{16,8},{24,16},{9,1},{17,9},{25,17},{10,2},{18,10},{26,18},{... | collective-permute-start | bytes 626696 | tf_op jit(solution)/shard_map/ppermute | solution.py:1122
  180.9 9.2 %collective-permute-start.21 = (f32[32,1024]{1,0:T(8,128)S(1)}, f32[32,1024]{1,0:T(8,128)S(1)}, u32[]{:S(2)}, u32[]{:S(2)}) collective-permute-start(f32[32,1024]{1,0:T(8,128)S(1)} %get-tuple-element.159), channel_id=1, source_target_pairs={{0,2},{2,4},{4,6},{6,0},{1,3},{3,5},{5,7},{7,1},{8,10},{10,12},{12... | collective-permute-start | bytes 393224 | tf_op jit(solution)/shard_map/ppermute | solution.py:1323
  293.9 21.8 %all-to-all-start.3 = ((f32[8,12,1280]{2,1,0:T(8,128)}), f32[8,12,1280]{2,1,0:T(8,128)S(1)}, u32[]{:S(2)}, u32[]{:S(2)}) async-start(f32[8,12,1280]{2,1,0:T(8,128)} %reshape.306), calls=%async_computation.4 | async-start | bytes 1310720 | tf_op jit(solution)/shard_map/all_to_all | solution.py:1400
  297.5 149.6 %reduce-scatter.8.cloned.1.call-start = ((), (), s32[]{:S(2)}) async-start(), calls=%async_computation.10 | async-start | bytes 7077888 | tf_op jit(solution)/shard_map/reduce_scatter | solution.py:1419
  341.0 107.5 %reduce-scatter.6.cloned.1.call-start = ((), (), s32[]{:S(2)}) async-start(), calls=%async_computation.9 | async-start | bytes 7077888 | tf_op jit(solution)/shard_map/reduce_scatter | solution.py:1420
  355.8 10.0 %collective-permute-start.25 = (f32[21,256,256]{2,1,0:T(8,128)}, f32[21,256,256]{2,1,0:T(8,128)}, u32[]{:S(2)}, u32[]{:S(2)}) collective-permute-start(f32[21,256,256]{2,1,0:T(8,128)} %gram.2), channel_id=1, source_target_pairs={{0,1},{1,0},{2,3},{3,2},{4,5},{5,4},{6,7},{7,6},{8,9},{9,8},{10,11... | collective-permute-start | bytes 16515080 | tf_op jit(solution)/shard_map/ppermute | solution.py:1411
  426.4 7.4 %collective-permute-start.26 = (f32[24,1536]{1,0:T(8,128)S(1)}, f32[24,1536]{1,0:T(8,128)S(1)}, u32[]{:S(2)}, u32[]{:S(2)}) collective-permute-start(f32[24,1536]{1,0:T(8,128)S(1)} %chain.1), channel_id=1, source_target_pairs={{0,1},{1,0},{2,3},{3,2},{4,5},{5,4},{6,7},{7,6},{8,9},{9,8},{10,11... | collective-permute-start | bytes 442376 | tf_op jit(solution)/shard_map/ppermute | solution.py:1431
  (97 other events, 1195.9 us)
Sparse Core Ops, SparseCore 0:
  25.8 54.6 all-gather.4
  145.6 84.7 reduce-scatter.3
  233.8 107.2 all-gather.6
  343.3 45.7 reduce-scatter.7
  391.3 41.7 reduce-scatter.5
where the time goes:
time: 464 us; the launch traced here: 458 us
  Pallas kernels  137 us (30%)
  blocking collectives  85.3 us (18%)
  waiting for transfers between devices  81.5 us (18%)
  starting transfers between devices  49.8 us (11%)
  local copies, waits for them, and re-layouts  46.6 us (10%)
  matrix products  25 us (5%)
  other arithmetic  16.9 us (4%)
  between operations  15.8 us (3%)
    pallas_call x1, Pallas kernels, chain(): pl.pallas_call(chain_kernel, out_shape=jax.ShapeDtypeStruct(pick.shape, F...  60.5 us
    all_to_all x1, blocking collectives, local(): lax.all_to_all(late_partial.reshape(16, team_count, LATE_COLS), ROWS, 0,...  34 us
    all_gather x1, waiting for transfers between devices, local(): lax.all_gather(momenta.astype(BF16), ('y', 'z', 'x')).reshape(4, D, BLOCK)  24.6 us
    unnamed x192, local copies, waits for them, and re-layouts  24 us
    pallas_call x2, Pallas kernels, gram(): pl.pallas_call(gram_kernel, in_specs=[pl.BlockSpec(memory_space=pltpu.SME...  22.4 us
    all_gather x1, blocking collectives, local(): vector = lax.all_gather(vector, TEAM).reshape(G, -1)  20.1 us
    all_gather x1, blocking collectives, local(): vector = jnp.sum(lax.all_gather(vector, ROWS), axis=0)  17.3 us
    dot_general x3, matrix products, dot(): lax.dot_general(a.astype(BF16), b.astype(BF16), (dims, ((), ())), preferr...  16.5 us
  transfers between devices with their start and end apart: 35, of which 19 were waited for; matrix products, arithmetic and copies ran while one was open for 12% of the time, Pallas kernels for 27%

commit v1 on v0

--- a/solution.py
+++ b/solution.py
@@ -616,66 +616,25 @@
         late_ref[0:EDGE, EG:] = edge_rows(following[...], taps_ref[...], edge_flags_ref[...])
 
 
+def finish_kernel(hidden_ref, cotangent_ref, d_normed_ref, mixed_ref, gain_ref, out_ref, grad_ref):
+    x = hidden_ref[...].astype(F32)
+    scale = lax.rsqrt(jnp.mean(x * x, axis=1, keepdims=True) + EPSILON)
+    unit = x * scale
+    d_unit = d_normed_ref[...] * gain_ref[...]
+    inner = jnp.mean(d_unit * unit, axis=1, keepdims=True)
+    grad_ref[...] = cotangent_ref[...].astype(F32) + scale * (d_unit - unit * inner)
+    out_ref[...] = (x + mixed_ref[...]).astype(BF16)
+
+
 def triangle(n):
     return [(i, j) for i in range(n // TILE) for j in range(i, n // TILE)]
 
 
-def gram_kernel(which_ref, x_ref, out_ref, held, total, in_sems, out_sems):
-    parts_of_x, n, _ = x_ref.shape
-    count = n // TILE
-    order = triangle(n)
-
-    def at(i):
-        return pl.ds(i * TILE, TILE)
-
-    def run(columns):
-        width = columns.stop - columns.start
-        arriving = [
-            pltpu.make_async_copy(
-                x_ref.at[y, :, columns], held.at[y, :, pl.ds(0, width)], in_sems.at[y]
-            )
-            for y in range(parts_of_x)
-        ]
-        leaving = []
-        for copy in arriving:
-            copy.start()
-        for y in range(0, parts_of_x, 2):
-            for copy in (arriving[y], arriving[y + 1]):
-                copy.wait()
-            for i in range(count):
-
-                def taken(rows):
-                    return jnp.concatenate(
-                        [held[y, rows, :width], held[y + 1, rows, :width]], axis=1
-                    )
-
-                product = dot(taken(at(i)), taken(pl.ds(i * TILE, n - i * TILE)), NT)
-                own = order.index((i, i))
-                for j in range(i, count):
-                    block = product[:, (j - i) * TILE : (j - i + 1) * TILE]
-                    b = own + j - i
-                    total[b] = block if y == 0 else total[b] + block
-                if y + 2 == parts_of_x:
-                    blocks = pl.ds(own, count - i)
-                    leaving.append(
-                        pltpu.make_async_copy(
-                            total.at[blocks], out_ref.at[blocks], out_sems.at[i]
-                        )
-                    )
-                    leaving[-1].start()
-        for copy in leaving:
-            copy.wait()
-
-    @pl.when(which_ref[0] == 1)
-    def _():
-        run(slice(0, IN_COLS))
-
-    @pl.when(which_ref[0] != 1)
-    def _():
-        run(slice(IN_COLS, BLOCK))
-
-
-def chain_kernel(own_ref, got_ref, pick_ref, t_ref, high, low, h_high, h_low, q_ref):
+def solve_kernel(
+    which_ref, x_ref, pick_ref, out_ref, total, high, low, h_high, h_low, q_ref, sems
+):
+    pieces = x_ref.shape[0]
+    slots = q_ref.shape[0]
     n = high.shape[0]
     count = n // TILE
     order = triangle(n)
@@ -685,12 +644,79 @@
 
     def times(a, b):
         return jnp.dot(a, b, preferred_element_type=F32)
+
+    def arriving(y, slot, columns):
+        width = columns.stop - columns.start
+        return pltpu.make_async_copy(
+            x_ref.at[y, :, columns], q_ref.at[slot, :, pl.ds(0, width)], sems.at[slot]
+        )
+
+    def gram(columns):
+        width = columns.stop - columns.start
+        for slot in range(slots):
+            arriving(slot, slot, columns).start()
+
+        def two(step, _):
+            slot = 2 * (step % (slots // 2))
+            for k in range(2):
+                arriving(2 * step + k, slot + k, columns).wait()
+
+            def taken(rows):
+                return jnp.concatenate(
+                    [q_ref[slot, rows, :width], q_ref[slot + 1, rows, :width]], axis=1
+                )
+
+            for i in range(count):
+                product = dot(taken(at(i)), taken(pl.ds(i * TILE, n - i * TILE)), NT)
+                for j in range(i, count):
+                    b = order.index((i, j))
+                    total[b] = total[b] + product[:, (j - i) * TILE : (j - i + 1) * TILE]
+
+            @pl.when(step < (pieces - slots) // 2)
+            def _():
+                for k in range(2):
+                    arriving(2 * step + slots + k, slot + k, columns).start()
+
+            return 0
+
+        lax.fori_loop(0, pieces // 2, two, 0)
+
+    def apply(columns, t):
+        width = columns.stop - columns.start
+        both = jnp.concatenate(parts(t), axis=0)
+        for slot in range(slots):
+            arriving(slot, slot, columns).start()
+
+        def one(y, _):
+            slot = y % slots
+            arriving(y, slot, columns).wait()
+            product = times(both, q_ref[slot, :, :width])
+            out_ref[y, :, :width] = product[: t.shape[0]] + product[t.shape[0] :]
+
+            @pl.when(y < pieces - slots)
+            def _():
+                arriving(y + slots, slot, columns).start()
+
+            return 0
+
+        lax.fori_loop(0, pieces, one, 0)
+
+    total[...] = jnp.zeros_like(total)
+    out_ref[...] = jnp.zeros_like(out_ref)
+
+    @pl.when(which_ref[0] == 1)
+    def _():
+        gram(slice(0, IN_COLS))
+
+    @pl.when(which_ref[0] != 1)
+    def _():
+        gram(slice(IN_COLS, BLOCK))
 
     diagonal = lax.broadcasted_iota(jnp.int32, (TILE, TILE), 0) == lax.broadcasted_iota(jnp.int32, (TILE, TILE), 1)
     square = jnp.zeros((1, 1), F32)
     for b, (i, j) in enumerate(order):
         if i == j:
-            square = square + jnp.sum(jnp.where(diagonal, own_ref[b] + got_ref[b], 0.0), keepdims=True)
+            square = square + jnp.sum(jnp.where(diagonal, total[b], 0.0), keepdims=True)
     inverse = 1.0 / (jnp.sqrt(square) + NORM_FLOOR)
     scale = inverse * inverse
 
@@ -707,7 +733,7 @@
             put(value[:, (j - i) * TILE : (j - i + 1) * TILE], i, j, top_ref, rest_ref)
 
     for b, (i, j) in enumerate(order):
-        put((own_ref[b] + got_ref[b]) * scale, i, j, high, low)
+        put(total[b] * scale, i, j, high, low)
 
     def polynomial(q):
         for i in range(count):
@@ -749,7 +775,15 @@
     t = POLY_FIRST * pick + POLY_SECOND * once + POLY_THIRD * last_gram(once)
     for step in reversed(range(NS_STEPS - 1)):
         t = multiplied(t, step)
-    t_ref[...] = t * inverse
+    t = t * inverse
+
+    @pl.when(which_ref[0] == 1)
+    def _():
+        apply(slice(0, IN_COLS), t)
+
+    @pl.when(which_ref[0] != 1)
+    def _():
+        apply(slice(IN_COLS, BLOCK), t)
 
 
 SMALL = pltpu.CompilerParams(vmem_limit_bytes=20 << 20)
@@ -1080,40 +1114,38 @@
     )(team, *got, conv, conv, v, v, v, v, dr, dv, d_edge, flags, edge_flags, taps)
 
 
-def gram(which, x):
-    count, n, _ = x.shape
-    blocks = len(triangle(n))
+def finish(hidden, cotangent, d_normed, mixed, gain):
+    count = hidden.shape[0]
     return pl.pallas_call(
-        gram_kernel,
-        in_specs=[pl.BlockSpec(memory_space=pltpu.SMEM), pl.BlockSpec(memory_space=pl.ANY)],
-        out_specs=pl.BlockSpec(memory_space=pl.ANY),
-        out_shape=shaped(blocks, TILE, TILE),
-        scratch_shapes=[
-            pltpu.VMEM((count, n, IN_COLS), BF16),
-            pltpu.VMEM((blocks, TILE, TILE), F32),
-            pltpu.SemaphoreType.DMA((count,)),
-            pltpu.SemaphoreType.DMA((n // TILE,)),
-        ],
-        compiler_params=LARGE,
-        cost_estimate=cost(n * n * count * BLOCK * 3 // 5, 14 << 20),
-        name="gram",
-    )(which.astype(jnp.int32).reshape(1), x)
-
-
-def chain(own, got, pick):
-    n = pick.shape[1]
-    whole = pl.BlockSpec(memory_space=pltpu.VMEM)
+        finish_kernel,
+        grid=(2,),
+        in_specs=[rows(D, count // 2)] * 4 + [spec((1, D))],
+        out_specs=[rows(D, count // 2)] * 2,
+        out_shape=[shaped(count, D, dtype=BF16), shaped(count, D)],
+        compiler_params=SMALL,
+        cost_estimate=cost(20 * count * D, 4 << 20),
+        name="finish",
+    )(hidden, cotangent, d_normed, mixed, gain)
+
+
+def solve(which, x, pick):
+    pieces, n, _ = x.shape
     return pl.pallas_call(
-        chain_kernel,
-        out_shape=jax.ShapeDtypeStruct(pick.shape, F32),
-        in_specs=[whole, whole, whole],
-        out_specs=whole,
-        scratch_shapes=[pltpu.VMEM((n, n), BF16)] * 4
-        + [pltpu.VMEM((NS_STEPS - 1, n, n), BF16)],
-        compiler_params=pltpu.CompilerParams(vmem_limit_bytes=52 << 20),
-        cost_estimate=cost(14 * n * n * n, 11 << 20),
-        name="chain",
-    )(own, got, pick)
+        solve_kernel,
+        out_shape=shaped(pieces, pick.shape[0], IN_COLS),
+        in_specs=[
+            pl.BlockSpec(memory_space=pltpu.SMEM),
+            pl.BlockSpec(memory_space=pl.ANY),
+            pl.BlockSpec(memory_space=pltpu.VMEM),
+        ],
+        out_specs=pl.BlockSpec(memory_space=pltpu.VMEM),
+        scratch_shapes=[pltpu.VMEM((len(triangle(n)), TILE, TILE), F32)]
+        + [pltpu.VMEM((n, n), BF16)] * 4
+        + [pltpu.VMEM((NS_STEPS - 1, n, n), BF16), pltpu.SemaphoreType.DMA((NS_STEPS - 1,))],
+        compiler_params=pltpu.CompilerParams(vmem_limit_bytes=62 << 20),
+        cost_estimate=cost(20 * n * n * n, 44 << 20),
+        name="solve",
+    )(which.astype(jnp.int32).reshape(1), x, pick)
 
 
 def summaries(packed, direction):
@@ -1332,9 +1364,19 @@
     )
     late_sum = jnp.sum(late_parts.astype(F32), axis=0)
 
+    ahead = MATRIX_MOMENTUM * momentum_block.astype(F32)
+    late_new = (ahead[:, EG:IN_COLS] + late_sum).astype(BF16)
+    late_new, ahead = lax.optimization_barrier((late_new, ahead))
+    momenta = jnp.concatenate(
+        [
+            (ahead[:, :EG] + early_sum[:, :EG]).astype(BF16),
+            late_new,
+            (ahead[:, IN_COLS:] + early_sum[:, EG:]).astype(BF16),
+        ],
+        axis=1,
+    )
     sums_block = jnp.concatenate([early_sum[:, :EG], late_sum, early_sum[:, EG:]], axis=1)
-    momenta = MATRIX_MOMENTUM * momentum_block.astype(F32) + sums_block
-    x_all = lax.all_gather(momenta.astype(BF16), ("y", "z", "x")).reshape(4, D, BLOCK)
+    x_all = lax.all_gather(momenta, TEAM + ROWS).reshape(G, D, BLOCK)
 
     late_back = lax.ppermute(
         late[TOKENS:], "x", [(s, s - 1) for s in range(1, lax.axis_size("x"))]
@@ -1404,49 +1446,38 @@
     in_momentum_new = MATRIX_MOMENTUM * in_momentum + in_grad
     out_momentum_new = MATRIX_MOMENTUM * out_momentum + out_grad
 
-    x_all, d_normed_part, mixed_part, vector_grad, in_grad = lax.optimization_barrier(
-        (x_all, d_normed_part, mixed_part, vector_grad, in_grad)
-    )
-    gram_sent = gram(ci == 1, x_all)
-    gram_got = lax.ppermute(gram_sent, "c", swap)
-    gram_own = gram(after(first, gram_sent), x_all)
     chip_row = (zi * 4 + xi) * team_count + yi * (2 * count)
     pick = (
         lax.broadcasted_iota(jnp.int32, (2 * count, D), 1)
         == lax.broadcasted_iota(jnp.int32, (2 * count, D), 0) + chip_row
     ).astype(F32)
-    t_own = chain(gram_own, gram_got, pick)
+    (
+        x_all, pick, d_normed_part, mixed_part,
+        vector_grad, vector_momentum_new, vector_new,
+        in_grad, in_momentum_new, out_grad, out_momentum_new,
+    ) = lax.optimization_barrier(
+        (
+            x_all, pick, d_normed_part, mixed_part,
+            vector_grad, vector_momentum_new, vector_new,
+            in_grad, in_momentum_new, out_grad, out_momentum_new,
+        )
+    )
+    steps = solve(first, x_all, pick)
     d_normed = lax.psum_scatter(d_normed_part, TEAM, scatter_dimension=0, tiled=True)
     mixed = lax.psum_scatter(mixed_part, TEAM, scatter_dimension=0, tiled=True)
-    hidden_own = hidden.astype(F32)
-    block_output = (hidden_own + mixed).astype(BF16)
-    scale_own = lax.rsqrt(jnp.mean(hidden_own * hidden_own, axis=-1, keepdims=True) + EPSILON)
-    unit_own = hidden_own * scale_own
-    d_unit = d_normed * norm_gain
-    d_hidden = scale_own * (
-        d_unit - unit_own * jnp.mean(d_unit * unit_own, axis=-1, keepdims=True)
-    )
-    input_grad = cotangent.astype(F32) + d_hidden
-
-    t_other = lax.ppermute(t_own, "c", swap)
-    t_in = jnp.where(first, t_own, t_other)
-    t_out = jnp.where(first, t_other, t_own)
-
-    def applied(t, x):
-        both = jnp.einsum(
-            "rk,ykn->yrn", jnp.concatenate(parts(t), axis=0), x, preferred_element_type=F32
-        )
-        return both[:, : 2 * count] + both[:, 2 * count :]
-
-    halves = jnp.concatenate(
-        [applied(t_in, x_all[:, :, :IN_COLS]), applied(t_out, x_all[:, :, IN_COLS:])], axis=2
-    )
-    half_own = lax.dynamic_slice_in_dim(halves, ci * count, count, 1)
-    half_sent = lax.dynamic_slice_in_dim(halves, (1 - ci) * count, count, 1)
-    half_got = lax.ppermute(half_sent, "c", swap)
-    both = jnp.stack(
-        [jnp.where(first, half_own, half_got), jnp.where(first, half_got, half_own)], axis=1
-    ).reshape(G, count, BLOCK)
+    block_output, input_grad = finish(hidden, cotangent, d_normed, mixed, norm_gain[None, :])
+
+    own_steps = lax.dynamic_slice_in_dim(steps, ci * count, count, 1)
+    got_steps = lax.ppermute(
+        lax.dynamic_slice_in_dim(steps, (1 - ci) * count, count, 1), "c", swap
+    )
+    both = jnp.concatenate(
+        [
+            jnp.where(first, own_steps, got_steps),
+            jnp.where(first, got_steps, own_steps)[:, :, : BLOCK - IN_COLS],
+        ],
+        axis=2,
+    )
     step_in, step_out = rows_of_blocks(both)
     in_weight_new = in_weight.astype(F32) - MATRIX_RATE * math.sqrt(PROJ / D) * step_in
     out_weight_new = out_weight.astype(F32) - MATRIX_RATE * math.sqrt(E / D) * step_out

time: 464 us -> 461 us (level)
  blocking collectives: 85.3 us -> 52.6 us
  starting transfers between devices: 49.8 us -> 73.9 us
  waiting for transfers between devices: 81.5 us -> 101 us
  matrix products: 25 us -> 16.6 us
  Pallas kernels: 137 us -> 129 us
    all_to_all x1 -> x0, blocking collectives: 34 us -> none  [local(): lax.all_to_all(late_partial.reshape(16, team_count, LATE_COLS), ROWS, 0,...]
    all_to_all x0 -> x1, waiting for transfers between devices: none -> 25.2 us  [local(): lax.all_to_all(late_partial.reshape(16, team_count, LATE_COLS), ROWS, 0,...]
    all_to_all x0 -> x1, starting transfers between devices: none -> 9.66 us  [local(): lax.all_to_all(late_partial.reshape(16, team_count, LATE_COLS), ROWS, 0,...]
    ppermute x3 -> x1, starting transfers between devices: 6.89 us -> 16.2 us  [local(): lax.ppermute(lax.dynamic_slice_in_dim(steps, (1 - ci) * count, count, 1),...]
    dot_general x2 -> x0, matrix products: 8.54 us -> none  [applied(): jnp.einsum('rk,ykn->yrn', jnp.concatenate(parts(t), axis=0), x, preferred...]
    pallas_call x3 -> x2, Pallas kernels: 82.9 us -> 74.9 us  [the longest x1 73.6 us: solve(): pl.pallas_call(solve_kernel, out_shape=shaped(pieces, pick.shape[0], IN_C...]
    unnamed x192 -> x196, local copies, waits for them, and re-layouts: 24 us -> 28.1 us
  transfers between devices with their start and end apart: 35 -> 34, of which waited for: 19 -> 16; matrix products, arithmetic and copies ran while one was open for 12% -> 11% of each run, Pallas kernels for 27% -> 26%
where the time goes in v1:
time: 461 us; the launch traced here: 454 us
  Pallas kernels  129 us (28%)
  waiting for transfers between devices  101 us (22%)
  starting transfers between devices  73.9 us (16%)
  blocking collectives  52.6 us (11%)
  local copies, waits for them, and re-layouts  47.7 us (10%)
  other arithmetic  16.7 us (4%)
  matrix products  16.6 us (4%)
  between operations  15.8 us (3%)
    pallas_call x1, Pallas kernels, solve(): pl.pallas_call(solve_kernel, out_shape=shaped(pieces, pick.shape[0], IN_C...  73.6 us
    unnamed x196, local copies, waits for them, and re-layouts  28.1 us
    all_to_all x1, waiting for transfers between devices, local(): lax.all_to_all(late_partial.reshape(16, team_count, LATE_COLS), ROWS, 0,...  25.2 us
    all_gather x1, waiting for transfers between devices, local(): x_all = lax.all_gather(momenta, TEAM + ROWS).reshape(G, D, BLOCK)  23.5 us
    all_gather x1, blocking collectives, local(): vector = lax.all_gather(vector, TEAM).reshape(G, -1)  21.3 us
    all_gather x1, blocking collectives, local(): vector = jnp.sum(lax.all_gather(vector, ROWS), axis=0)  17.4 us
    dot_general x3, matrix products, dot(): lax.dot_general(a.astype(BF16), b.astype(BF16), (dims, ((), ())), preferr...  16.6 us
    ppermute x1, starting transfers between devices, local(): lax.ppermute(lax.dynamic_slice_in_dim(steps, (1 - ci) * count, count, 1),...  16.2 us
  transfers between devices with their start and end apart: 34, of which 16 were waited for; matrix products, arithmetic and copies ran while one was open for 11% of the time, Pallas kernels for 26%

profile of v1, /device:TPU:1, one launch (start us, length us, event | category | flops | bytes accessed | tf_op | source)
XLA Modules:
  0.0 454.0 jit_solution(7926213683685530543)
XLA Ops:
  10.3 13.9 %all_to_all.20 = bf16[8,12,1536]{2,1,0:T(8,128)(2,1)S(1)} all-to-all(bf16[8,12,1536]{2,1,0:T(8,128)(2,1)S(1)} %bitcast.136), channel_id=1, replica_groups=mesh['z'=4,'x'=4,'y'=4,'c'=2] {'y','c'}, dimensions={0} | all-to-all | bytes 589824 | tf_op jit(solution)/shard_map/all_to_all | solution.py:1238
  30.7 5.5 %all-to-all-start.1 = ((bf16[8,12,1280]{2,1,0:T(8,128)(2,1)}), bf16[8,12,1280]{2,1,0:T(8,128)(2,1)S(1)}, u32[]{:S(2)}, u32[]{:S(2)}) async-start(bf16[8,12,1280]{2,1,0:T(8,128)(2,1)} %bitcast.2), calls=%async_computation.1 | async-start | bytes 655360 | tf_op jit(solution)/shard_map/all_to_all | solution.py:1243
  36.5 14.0 %all-to-all-done.1 = bf16[8,12,1280]{2,1,0:T(8,128)(2,1)S(1)} async-done(((bf16[8,12,1280]{2,1,0:T(8,128)(2,1)}), bf16[8,12,1280]{2,1,0:T(8,128)(2,1)S(1)}, u32[]{:S(2)}, u32[]{:S(2)}) %all-to-all-start.1) | async-done | bytes 245792 | tf_op jit(solution)/shard_map/all_to_all | solution.py:1243
  63.2 4.0 collective-permute-start.4
  70.6 6.2 %collective-permute-done.6 = bf16[128,1536]{1,0:T(8,128)(2,1)} collective-permute-done((bf16[128,1536]{1,0:T(8,128)(2,1)S(1)}, bf16[128,1536]{1,0:T(8,128)(2,1)}, u32[]{:S(2)}, u32[]{:S(2)}) %collective-permute-start.6) | collective-permute-done | bytes 393248 | tf_op jit(solution)/shard_map/ppermute | solution.py:1190
  84.3 9.5 %project.1 = (bf16[1040,1536]{1,0:T(8,128)(2,1)S(1)}, f32[1040,384]{1,0:T(8,128)S(1)}, f32[1040,640]{1,0:T(8,128)S(1)}, f32[1040,128]{1,0:T(8,128)S(1)}) custom-call(s32[2]{0:T(128)S(1)} %pad_add_fusion.core_ref, bf16[4,128,1664]{2,1,0:T(8,128)(2,1)S(1)} %copy-done.16, bf16[4,128,1664]{2,1,0:T(8,128)(2,1)} %collective-permute-done.3.other_ref, ...), custom_call_target="tpu_custom_call" | custom-call | flops 3680501760 | bytes 16777216 | tf_op jit(solution)/shard_map/project/pallas_call | solution.py:836
  93.9 8.6 %forward.1 = (f32[1024,640]{1,0:T(8,128)S(1)}, f32[1024,128]{1,0:T(8,128)S(1)}, f32[1024,128]{1,0:T(8,128)S(1)}, f32[1024,384]{1,0:T(8,128)S(1)}, f32[8,128,384]...) custom-call(f32[1040,640]{1,0:T(8,128)S(1)} %get-tuple-element.95.v_ref.before_ref.refs_2_, ...), custom_call_target="tpu_custom_call" | custom-call | flops 3221225472 | bytes 14680064 | tf_op jit(solution)/shard_map/forward/pallas_call | solution.py:906
  106.5 4.4 collective-permute-start.11
  112.2 4.7 %incoming.1 = (bf16[1024,1536]{1,0:T(8,128)(2,1)S(1)}, f32[1024,384]{1,0:T(8,128)S(1)}) custom-call(s32[2]{0:T(128)S(1)} %pad_add_fusion.core_ref, bf16[4,128,1536]{2,1,0:T(8,128)(2,1)} %pad_maximum_fusion.1.own_ref, bf16[4,128,1536]{2,1,0:T(8,128)(2,1)} %collective-permute-done.9.other_ref, bf16[1536,1536]{1,0:T(8,128)(2,1)S(1)} %bitcast.105), custom_call_target="tpu_custom_call" | custom-call | flops 1207959552 | bytes 9437184 | tf_op jit(solution)/shard_map/incoming/pallas_call | solution.py:868
  128.5 4.2 gate.1
  136.3 5.1 %early.1 = bf16[1536,768]{1,0:T(8,128)(2,1)S(1)} custom-call(bf16[1040,1536]{1,0:T(8,128)(2,1)S(1)} %get-tuple-element.94.normed_ref, bf16[1024,1536]{1,0:T(8,128)(2,1)S(1)} %get-tuple-element.118.q_ref, bf16[1024,384]{1,0:T(8,128)(2,1)S(1)} %get-tuple-element.142.dz_ref, bf16[1024,384]{1,0:T(8,128)(2,1)S(1)} %get-tuple-element.145.gated_ref), custom_call_target="tpu_custom_call" | custom-call | flops 2415919104 | bytes 13631488 | tf_op jit(solution)/shard_map/early/pallas_call | solution.py:888
  154.2 5.8 %inner.1 = (f32[1024,384]{1,0:T(8,128)S(1)}, f32[1024,256]{1,0:T(8,128)S(1)}) custom-call(f32[1024,384]{1,0:T(8,128)S(1)} %copy-done.20, f32[1024,640]{1,0:T(8,128)S(1)} %copy-done.1, f32[1024,128]{1,0:T(8,128)S(1)} %copy-done.38, f32[1024,128]{1,0:T(8,128)S(1)} %copy-done.9, f32[1024,128]{1,0:T(8,128)S(1)} %pad.44.flags_ref.refs_9_, f32[8,128]{1,0:T(8,128)S(1)} %bitcast.115), custom_call_target="tpu_custom_call" | custom-call | flops 3221225472 | bytes 9437184 | tf_op jit(solution)/shard_map/inner/pallas_call | solution.py:991
  161.7 11.2 %backward.1 = (bf16[1024,384]{1,0:T(8,128)(2,1)S(1)}, bf16[16,384]{1,0:T(8,128)(2,1)S(1)}, f32[128,1024]{1,0:T(8,128)S(1)}, f32[128,1024]{1,0:T(8,128)}, f32[102...) custom-call(s32[2]{0:T(128)S(1)} %pad_add_fusion.core_ref, ...), custom_call_target="tpu_custom_call" | custom-call | flops 1610612736 | bytes 20971520 | tf_op jit(solution)/shard_map/backward/pallas_call | solution.py:1010
  198.9 9.7 %all-to-all-start.2 = ((bf16[16,96,512]{2,1,0:T(8,128)(2,1)}), bf16[16,96,512]{2,1,0:T(8,128)(2,1)S(1)}, u32[]{:S(2)}, u32[]{:S(2)}) async-start(bf16[16,96,512]{2,1,0:T(8,128)(2,1)} %bitcast.39), calls=%async_computation.2 | async-start | bytes 3145728 | tf_op jit(solution)/shard_map/all_to_all | solution.py:1362
  208.8 25.2 %all-to-all-done.2 = bf16[16,96,512]{2,1,0:T(8,128)(2,1)S(1)} async-done(((bf16[16,96,512]{2,1,0:T(8,128)(2,1)}), bf16[16,96,512]{2,1,0:T(8,128)(2,1)S(1)}, u32[]{:S(2)}, u32[]{:S(2)}) %all-to-all-start.2) | async-done | bytes 1572896 | tf_op jit(solution)/shard_map/all_to_all | solution.py:1362
  248.4 7.3 %multiply_reduce_fusion = (f32[1536]{0:T(1024)S(1)}, f32[1024,1536]{1,0:T(8,128)}) fusion(bf16[1040,1536]{1,0:T(8,128)(2,1)} %copy-done.13, bf16[1536,6]{1,0:T(8,128)(2,1)S(1)} %slice-done.4, bf16[1536,32]{1,0:T(8,128)(2,1)S(1)} %copy-done.65, bf16[1536,768]{1,0:T(8,128)(2,1)S(1)} %slice-done.3, bf16[896]{0:T(1024)(128)(2,1)} %pad.63.clone, ...), kind=kOutput, calls=%fused_computation.1 | convolution fusion | flops 2839804416 | bytes 13756160 | tf_op jit(solution)/shard_map/dot_general | solution.py:58
  255.7 17.4 %all_gather.21 = f32[16,32,128]{2,1,0:T(8,128)S(1)} all-gather(f32[1,32,128]{2,1,0:T(8,128)S(1)} %pad_bitcast_fusion), channel_id=1, replica_groups=mesh['z'=4,'x'=4,'y'=4,'c'=2] {'z','x'}, dimensions={0}, use_global_device_ids=true | all-gather | bytes 278528 | tf_op jit(solution)/shard_map/all_gather | solution.py:1420
  273.2 21.3 %all-gather.1 = f32[256,128]{1,0:T(8,128)S(1)} all-gather(f32[32,128]{1,0:T(8,128)S(1)} %reduce_sum.38), channel_id=3, replica_groups=mesh['z'=4,'x'=4,'y'=4,'c'=2] {'y','c'}, dimensions={0}, use_global_device_ids=true | all-gather | bytes 147456 | tf_op jit(solution)/shard_map/all_gather | solution.py:1421
  297.0 4.6 %all-to-all-start.3 = ((f32[8,12,1280]{2,1,0:T(8,128)}), f32[8,12,1280]{2,1,0:T(8,128)S(1)}, u32[]{:S(2)}, u32[]{:S(2)}) async-start(f32[8,12,1280]{2,1,0:T(8,128)} %reshape.286), calls=%async_computation.4 | async-start | bytes 1310720 | tf_op jit(solution)/shard_map/all_to_all | solution.py:1442
  301.6 5.8 %fusion.13 = f32[1024,1536]{1,0:T(8,128)} fusion(bf16[1024,384]{1,0:T(8,128)(2,1)S(1)} %copy-done.12, bf16[1536,1536]{1,0:T(8,128)(2,1)} %all-gather.5.cloned.1.call-done.w_ref), kind=kOutput, calls=%fused_computation.19 | convolution fusion | flops 1207959552 | bytes 8257536 | tf_op jit(solution)/shard_map/dot_general | solution.py:58
  307.5 12.3 %all-to-all-done.3 = f32[8,12,1280]{2,1,0:T(8,128)S(1)} async-done(((f32[8,12,1280]{2,1,0:T(8,128)}), f32[8,12,1280]{2,1,0:T(8,128)S(1)}, u32[]{:S(2)}, u32[]{:S(2)}) %all-to-all-start.3) | async-done | bytes 491552 | tf_op jit(solution)/shard_map/all_to_all | solution.py:1442
  322.5 23.5 %all-gather.7.cloned.1.call-done = bf16[12288,1280]{1,0:T(8,128)(2,1)} async-done(((bf16[96,1280]{1,0:T(8,128)(2,1)}), bf16[12288,1280]{1,0:T(8,128)(2,1)}) %all-gather.7.cloned.1.call-update) | async-done | bytes 31457296 | tf_op jit(solution)/shard_map/all_gather | solution.py:1379
  346.6 73.6 %solve.1 = f32[8,24,896]{2,1,0:T(8,128)} custom-call(s32[1]{0:T(128)} %bitcast.46.which_ref, bf16[8,1536,1280]{2,1,0:T(8,128)(2,1)} %bitcast.165, f32[24,1536]{1,0:T(8,128)} %fusion.20.pick_ref), custom_call_target="tpu_custom_call" | custom-call | flops 72477573120 | bytes 46137344 | tf_op jit(solution)/shard_map/solve/pallas_call | solution.py:1133
  421.4 16.2 %collective-permute-start.25 = (f32[8,12,896]{2,1,0:T(8,128)S(1)}, f32[8,12,896]{2,1,0:T(8,128)S(1)}, u32[]{:S(2)}, u32[]{:S(2)}) collective-permute-start(f32[8,12,896]{2,1,0:T(8,128)S(1)} %constant_dynamic-slice_fusion), channel_id=1, source_target_pairs={{0,1},{1,0},{2,3},{3,2},{4,5},{5,4},{6,7},{7,6},{8,9},{9,8},{10,11... | collective-permute-start | bytes 1032200 | tf_op jit(solution)/shard_map/ppermute | solution.py:1471
  (436 shorter events, 124.4 us)
Async XLA Ops:
  7.2 73.4 %all-gather.5.cloned.1.call-start = ((), (), s32[]{:S(2)}) async-start(), calls=%async_computation.7 | async-start | bytes 5013504 | tf_op jit(solution)/shard_map/all_gather | solution.py:1239
  25.2 26.1 %collective-permute-start = (bf16[128,1664]{1,0:T(8,128)(2,1)S(1)}, bf16[128,1664]{1,0:T(8,128)(2,1)S(1)}, u32[]{:S(2)}, u32[]{:S(2)}) collective-permute-start(bf16[128,1664]{1,0:T(8,128)(2,1)S(1)} %fusion.16), channel_id=1, source_target_pairs={{0,2},{2,4},{4,6},{6,0},{1,3},{3,5},{5,7},{7,1},{8,10},{10,12},{12... | collective-permute-start | bytes 1277960 | tf_op jit(solution)/shard_map/ppermute | solution.py:1190
  25.5 25.7 %collective-permute-start.1 = (bf16[128,1664]{1,0:T(8,128)(2,1)S(1)}, bf16[128,1664]{1,0:T(8,128)(2,1)S(1)}, u32[]{:S(2)}, u32[]{:S(2)}) collective-permute-start(bf16[128,1664]{1,0:T(8,128)(2,1)S(1)} %fusion.16), channel_id=1, source_target_pairs={{0,4},{2,6},{4,0},{6,2},{1,5},{3,7},{5,1},{7,3},{8,12},{10,14},{12... | collective-permute-start | bytes 1277960 | tf_op jit(solution)/shard_map/ppermute | solution.py:1190
  27.3 23.9 %collective-permute-start.2 = (bf16[128,1664]{1,0:T(8,128)(2,1)S(1)}, bf16[128,1664]{1,0:T(8,128)(2,1)S(1)}, u32[]{:S(2)}, u32[]{:S(2)}) collective-permute-start(bf16[128,1664]{1,0:T(8,128)(2,1)S(1)} %fusion.16), channel_id=1, source_target_pairs={{0,6},{2,0},{4,2},{6,4},{1,7},{3,1},{5,3},{7,5},{8,14},{10,8},{12,... | collective-permute-start | bytes 1277960 | tf_op jit(solution)/shard_map/ppermute | solution.py:1190
  30.7 19.7 %all-to-all-start.1 = ((bf16[8,12,1280]{2,1,0:T(8,128)(2,1)}), bf16[8,12,1280]{2,1,0:T(8,128)(2,1)S(1)}, u32[]{:S(2)}, u32[]{:S(2)}) async-start(bf16[8,12,1280]{2,1,0:T(8,128)(2,1)} %bitcast.2), calls=%async_computation.1 | async-start | bytes 655360 | tf_op jit(solution)/shard_map/all_to_all | solution.py:1243
  36.2 198.0 %reduce-scatter.4.cloned.1.call-start = ((), (), s32[]{:S(2)}) async-start(), calls=%async_computation.8 | async-start | bytes 2506752 | tf_op jit(solution)/shard_map/reduce_scatter | solution.py:1341
  54.8 15.8 %collective-permute-start.5 = (bf16[128,1536]{1,0:T(8,128)(2,1)S(1)}, bf16[128,1536]{1,0:T(8,128)(2,1)}, u32[]{:S(2)}, u32[]{:S(2)}) collective-permute-start(bf16[128,1536]{1,0:T(8,128)(2,1)S(1)} %copy-done.23), channel_id=1, source_target_pairs={{0,2},{2,4},{4,6},{6,0},{1,3},{3,5},{5,7},{7,1},{8,10},{10,12},{12... | collective-permute-start | bytes 1179656 | tf_op jit(solution)/shard_map/ppermute | solution.py:1190
  55.6 21.2 %collective-permute-start.6 = (bf16[128,1536]{1,0:T(8,128)(2,1)S(1)}, bf16[128,1536]{1,0:T(8,128)(2,1)}, u32[]{:S(2)}, u32[]{:S(2)}) collective-permute-start(bf16[128,1536]{1,0:T(8,128)(2,1)S(1)} %copy-done.23), channel_id=1, source_target_pairs={{0,4},{2,6},{4,0},{6,2},{1,5},{3,7},{5,1},{7,3},{8,12},{10,14},{12... | collective-permute-start | bytes 1179656 | tf_op jit(solution)/shard_map/ppermute | solution.py:1190
  59.1 17.8 %collective-permute-start.7 = (bf16[128,1536]{1,0:T(8,128)(2,1)S(1)}, bf16[128,1536]{1,0:T(8,128)(2,1)}, u32[]{:S(2)}, u32[]{:S(2)}) collective-permute-start(bf16[128,1536]{1,0:T(8,128)(2,1)S(1)} %copy-done.23), channel_id=1, source_target_pairs={{0,6},{2,0},{4,2},{6,4},{1,7},{3,1},{5,3},{7,5},{8,14},{10,8},{12,... | collective-permute-start | bytes 1179656 | tf_op jit(solution)/shard_map/ppermute | solution.py:1190
  60.9 6.3 %collective-permute-start.8 = (f32[128]{0:T(128)S(1)}, f32[128]{0:T(128)S(1)}, u32[]{:S(2)}, u32[]{:S(2)}) collective-permute-start(f32[128]{0:T(128)S(1)} %slice.232), channel_id=1, source_target_pairs={{8,0},{16,8},{24,16},{9,1},{17,9},{25,17},{10,2},{18,10},{26,18},{... | collective-permute-start | bytes 1544 | tf_op jit(solution)/shard_map/ppermute | solution.py:1286
  79.5 32.7 %collective-permute-start.9 = (bf16[4,128,1536]{2,1,0:T(8,128)(2,1)}, bf16[4,128,1536]{2,1,0:T(8,128)(2,1)}, u32[]{:S(2)}, u32[]{:S(2)}) collective-permute-start(bf16[4,128,1536]{2,1,0:T(8,128)(2,1)} %pad_maximum_fusion.1.own_ref), channel_id=1, source_target_pairs={{0,1},{1,0},{2,3},{3,2},{4,5},{5,4},{6,7},{7,6},{8,9},{9,8},{10,11... | collective-permute-start | bytes 4718600 | tf_op jit(solution)/shard_map/ppermute | solution.py:1326
  103.3 13.6 %collective-permute-start.10 = (f32[136,384]{1,0:T(8,128)S(1)}, f32[136,384]{1,0:T(8,128)S(1)}, u32[]{:S(2)}, u32[]{:S(2)}) collective-permute-start(f32[136,384]{1,0:T(8,128)S(1)} %get-tuple-element.111.final_ref), channel_id=1, source_target_pairs={{0,8},{8,16},{16,24},{1,9},{9,17},{17,25},{2,10},{10,18},{18,26},{... | collective-permute-start | bytes 626696 | tf_op jit(solution)/shard_map/ppermute | solution.py:1154
  106.5 10.4 %collective-permute-start.11 = (f32[136,384]{1,0:T(8,128)S(1)}, f32[136,384]{1,0:T(8,128)S(1)}, u32[]{:S(2)}, u32[]{:S(2)}) collective-permute-start(f32[136,384]{1,0:T(8,128)S(1)} %get-tuple-element.111.final_ref), channel_id=1, source_target_pairs={{0,16},{8,24},{1,17},{9,25},{2,18},{10,26},{3,19},{11,27},{4,20},{... | collective-permute-start | bytes 626696 | tf_op jit(solution)/shard_map/ppermute | solution.py:1154
  110.8 7.8 %collective-permute-start.12 = (f32[136,384]{1,0:T(8,128)S(1)}, f32[136,384]{1,0:T(8,128)S(1)}, u32[]{:S(2)}, u32[]{:S(2)}) collective-permute-start(f32[136,384]{1,0:T(8,128)S(1)} %get-tuple-element.111.final_ref), channel_id=1, source_target_pairs={{0,24},{1,25},{2,26},{3,27},{4,28},{5,29},{6,30},{7,31},{32,56},{3... | collective-permute-start | bytes 626696 | tf_op jit(solution)/shard_map/ppermute | solution.py:1154
  144.6 15.4 %collective-permute-start.17 = (f32[136,384]{1,0:T(8,128)}, f32[136,384]{1,0:T(8,128)S(1)}, u32[]{:S(2)}, u32[]{:S(2)}) collective-permute-start(f32[136,384]{1,0:T(8,128)} %copy-done.48), channel_id=1, source_target_pairs={{8,0},{16,8},{24,16},{9,1},{17,9},{25,17},{10,2},{18,10},{26,18},{... | collective-permute-start | bytes 626696 | tf_op jit(solution)/shard_map/ppermute | solution.py:1154
  146.3 13.7 %collective-permute-start.18 = (f32[136,384]{1,0:T(8,128)}, f32[136,384]{1,0:T(8,128)S(1)}, u32[]{:S(2)}, u32[]{:S(2)}) collective-permute-start(f32[136,384]{1,0:T(8,128)} %copy-done.48), channel_id=1, source_target_pairs={{16,0},{24,8},{17,1},{25,9},{18,2},{26,10},{19,3},{27,11},{20,4},{... | collective-permute-start | bytes 626696 | tf_op jit(solution)/shard_map/ppermute | solution.py:1154
  147.6 14.0 %collective-permute-start.19 = (f32[136,384]{1,0:T(8,128)}, f32[136,384]{1,0:T(8,128)S(1)}, u32[]{:S(2)}, u32[]{:S(2)}) collective-permute-start(f32[136,384]{1,0:T(8,128)} %copy-done.48), channel_id=1, source_target_pairs={{24,0},{25,1},{26,2},{27,3},{28,4},{29,5},{30,6},{31,7},{56,32},{5... | collective-permute-start | bytes 626696 | tf_op jit(solution)/shard_map/ppermute | solution.py:1154
  181.3 9.1 %collective-permute-start.22 = (f32[32,1024]{1,0:T(8,128)S(1)}, f32[32,1024]{1,0:T(8,128)S(1)}, u32[]{:S(2)}, u32[]{:S(2)}) collective-permute-start(f32[32,1024]{1,0:T(8,128)S(1)} %get-tuple-element.179), channel_id=1, source_target_pairs={{0,4},{2,6},{4,0},{6,2},{1,5},{3,7},{5,1},{7,3},{8,12},{10,14},{12... | collective-permute-start | bytes 393224 | tf_op jit(solution)/shard_map/ppermute | solution.py:1355
  198.9 35.0 %all-to-all-start.2 = ((bf16[16,96,512]{2,1,0:T(8,128)(2,1)}), bf16[16,96,512]{2,1,0:T(8,128)(2,1)S(1)}, u32[]{:S(2)}, u32[]{:S(2)}) async-start(bf16[16,96,512]{2,1,0:T(8,128)(2,1)} %bitcast.39), calls=%async_computation.2 | async-start | bytes 3145728 | tf_op jit(solution)/shard_map/all_to_all | solution.py:1362
  208.6 137.4 %all-gather.7.cloned.1.call-start = ((), (), s32[]{:S(2)}) async-start(), calls=%async_computation.11 | async-start | bytes 31703040 | tf_op jit(solution)/shard_map/all_gather | solution.py:1379
  297.0 22.8 %all-to-all-start.3 = ((f32[8,12,1280]{2,1,0:T(8,128)}), f32[8,12,1280]{2,1,0:T(8,128)S(1)}, u32[]{:S(2)}, u32[]{:S(2)}) async-start(f32[8,12,1280]{2,1,0:T(8,128)} %reshape.286), calls=%async_computation.4 | async-start | bytes 1310720 | tf_op jit(solution)/shard_map/all_to_all | solution.py:1442
  301.6 142.1 %reduce-scatter.6.cloned.1.call-start = ((), (), s32[]{:S(2)}) async-start(), calls=%async_computation.9 | async-start | bytes 7077888 | tf_op jit(solution)/shard_map/reduce_scatter | solution.py:1466
  346.0 97.7 %reduce-scatter.8.cloned.1.call-start = ((), (), s32[]{:S(2)}) async-start(), calls=%async_computation.10 | async-start | bytes 7077888 | tf_op jit(solution)/shard_map/reduce_scatter | solution.py:1467
  421.4 17.6 %collective-permute-start.25 = (f32[8,12,896]{2,1,0:T(8,128)S(1)}, f32[8,12,896]{2,1,0:T(8,128)S(1)}, u32[]{:S(2)}, u32[]{:S(2)}) collective-permute-start(f32[8,12,896]{2,1,0:T(8,128)S(1)} %constant_dynamic-slice_fusion), channel_id=1, source_target_pairs={{0,1},{1,0},{2,3},{3,2},{4,5},{5,4},{6,7},{7,6},{8,9},{9,8},{10,11... | collective-permute-start | bytes 1032200 | tf_op jit(solution)/shard_map/ppermute | solution.py:1471
  (99 other events, 1017.2 us)
Sparse Core Ops, SparseCore 0:
  25.1 54.6 all-gather.4
  144.8 87.2 reduce-scatter.3
  236.1 109.8 all-gather.6
  348.2 41.0 reduce-scatter.5
  391.5 42.1 reduce-scatter.7

commit v2 on v1

--- a/solution.py
+++ b/solution.py
@@ -550,8 +550,6 @@
     before_b_ref,
     before_c_ref,
     dr_ref,
-    dv_ref,
-    d_edge_ref,
     flags_ref,
     edge_flags_ref,
     taps_ref,
@@ -602,8 +600,7 @@
                 * flags[:, AHEAD + lag : AHEAD + lag + 1]
             )
         following[...] = d_conv[0:8]
-        late_ref[at, :EG] = dv_ref[at, :]
-        late_ref[at, EG:] = (dv + pltpu.roll(dr_ref[at, :], BG, 1)).astype(BF16)
+        late_ref[at, :] = (dv + pltpu.roll(dr_ref[at, :], BG, 1)).astype(BF16)
 
     @pl.when(step < STEPS)
     def _():
@@ -612,8 +609,7 @@
 
     @pl.when(step == STEPS)
     def _():
-        late_ref[0:EDGE, :EG] = d_edge_ref[...]
-        late_ref[0:EDGE, EG:] = edge_rows(following[...], taps_ref[...], edge_flags_ref[...])
+        late_ref[0:EDGE, :] = edge_rows(following[...], taps_ref[...], edge_flags_ref[...])
 
 
 def finish_kernel(hidden_ref, cotangent_ref, d_normed_ref, mixed_ref, gain_ref, out_ref, grad_ref):
@@ -631,7 +627,7 @@
 
 
 def solve_kernel(
-    which_ref, x_ref, pick_ref, out_ref, total, high, low, h_high, h_low, q_ref, sems
+    which_ref, x_ref, pick_ref, own_ref, other_ref, total, high, low, h_high, h_low, q_ref, sems
 ):
     pieces = x_ref.shape[0]
     slots = q_ref.shape[0]
@@ -681,7 +677,8 @@
 
         lax.fori_loop(0, pieces // 2, two, 0)
 
-    def apply(columns, t):
+    def apply(columns, t, core):
+        half = t.shape[0] // 2
         width = columns.stop - columns.start
         both = jnp.concatenate(parts(t), axis=0)
         for slot in range(slots):
@@ -691,7 +688,9 @@
             slot = y % slots
             arriving(y, slot, columns).wait()
             product = times(both, q_ref[slot, :, :width])
-            out_ref[y, :, :width] = product[: t.shape[0]] + product[t.shape[0] :]
+            product = product[: t.shape[0]] + product[t.shape[0] :]
+            own_ref[y, :, :width] = product[core * half : (core + 1) * half]
+            other_ref[y, :, :width] = product[(1 - core) * half : (2 - core) * half]
 
             @pl.when(y < pieces - slots)
             def _():
@@ -702,7 +701,8 @@
         lax.fori_loop(0, pieces, one, 0)
 
     total[...] = jnp.zeros_like(total)
-    out_ref[...] = jnp.zeros_like(out_ref)
+    own_ref[...] = jnp.zeros_like(own_ref)
+    other_ref[...] = jnp.zeros_like(other_ref)
 
     @pl.when(which_ref[0] == 1)
     def _():
@@ -779,11 +779,11 @@
 
     @pl.when(which_ref[0] == 1)
     def _():
-        apply(slice(0, IN_COLS), t)
+        apply(slice(0, IN_COLS), t, 0)
 
     @pl.when(which_ref[0] != 1)
     def _():
-        apply(slice(IN_COLS, BLOCK), t)
+        apply(slice(IN_COLS, BLOCK), t, 1)
 
 
 SMALL = pltpu.CompilerParams(vmem_limit_bytes=20 << 20)
@@ -1069,7 +1069,7 @@
     )
 
 
-def shared(team, got, conv, v, dr, dv, d_edge, flags, edge_flags, taps):
+def shared(team, got, conv, v, dr, flags, edge_flags, taps):
     def turned(step):
         return jnp.maximum(STEPS - 1 - step, 0)
 
@@ -1096,22 +1096,20 @@
             before(b),
             before(c_block),
             lanes_of(0),
-            spec((SPAN, EG), lambda c: (turned(c), 0)),
-            spec((EDGE, EG)),
             lanes_of(0),
             spec((8, LANES)),
             spec((8, LANES)),
         ],
         out_specs=[
-            spec((SPAN, LATE_COLS), lambda c: (jnp.where(c == STEPS, STEPS, turned(c)), 0)),
+            spec((SPAN, LANES), lambda c: (jnp.where(c == STEPS, STEPS, turned(c)), 0)),
             spec((8, LANES)),
         ],
-        out_shape=[shaped(TOKENS + EDGE, LATE_COLS, dtype=BF16), shaped(8, LANES)],
+        out_shape=[shaped(TOKENS + EDGE, LANES, dtype=BF16), shaped(8, LANES)],
         scratch_shapes=[pltpu.VMEM((8, LANES), F32)],
         compiler_params=SMALL,
         cost_estimate=cost(1 << 27, 6 << 20),
         name="shared",
-    )(team, *got, conv, conv, v, v, v, v, dr, dv, d_edge, flags, edge_flags, taps)
+    )(team, *got, conv, conv, v, v, v, v, dr, flags, edge_flags, taps)
 
 
 def finish(hidden, cotangent, d_normed, mixed, gain):
@@ -1122,7 +1120,7 @@
         in_specs=[rows(D, count // 2)] * 4 + [spec((1, D))],
         out_specs=[rows(D, count // 2)] * 2,
         out_shape=[shaped(count, D, dtype=BF16), shaped(count, D)],
-        compiler_params=SMALL,
+        compiler_params=pltpu.CompilerParams(vmem_limit_bytes=60 << 20),
         cost_estimate=cost(20 * count * D, 4 << 20),
         name="finish",
     )(hidden, cotangent, d_normed, mixed, gain)
@@ -1132,13 +1130,13 @@
     pieces, n, _ = x.shape
     return pl.pallas_call(
         solve_kernel,
-        out_shape=shaped(pieces, pick.shape[0], IN_COLS),
+        out_shape=[shaped(pieces, pick.shape[0] // 2, IN_COLS)] * 2,
         in_specs=[
             pl.BlockSpec(memory_space=pltpu.SMEM),
             pl.BlockSpec(memory_space=pl.ANY),
             pl.BlockSpec(memory_space=pltpu.VMEM),
         ],
-        out_specs=pl.BlockSpec(memory_space=pltpu.VMEM),
+        out_specs=[pl.BlockSpec(memory_space=pltpu.VMEM)] * 2,
         scratch_shapes=[pltpu.VMEM((len(triangle(n)), TILE, TILE), F32)]
         + [pltpu.VMEM((n, n), BF16)] * 4
         + [pltpu.VMEM((NS_STEPS - 1, n, n), BF16), pltpu.SemaphoreType.DMA((NS_STEPS - 1,))],
@@ -1194,6 +1192,13 @@
 def team_sum(values):
     values = values + lax.ppermute(values, "c", [(0, 1), (1, 0)])
     return sum(along_y(values))
+
+
+def summands(normed, gradient):
+    part = dot(normed, gradient, TN).astype(BF16)
+    return lax.all_to_all(
+        part.reshape(16, D // 16, part.shape[1]), ROWS, 0, 0, tiled=True
+    )
 
 
 def after(value, *others):
@@ -1355,14 +1360,15 @@
         lax.ppermute(piece_for(k), "y", [(s, (s + k) % size_y) for s in range(size_y)])
         for k in range(1, size_y)
     ]
-    late, shared_sums = shared(
-        team.reshape(1), d_bc_got, conv, v, dr, dv, d_edge, flags, edge_flags, taps_shared
-    )
-    late_partial = dot(normed, late, TN).astype(BF16)
-    late_parts = lax.all_to_all(
-        late_partial.reshape(16, team_count, LATE_COLS), ROWS, 0, 0, tiled=True
-    )
-    late_sum = jnp.sum(late_parts.astype(F32), axis=0)
+    late_x = jnp.concatenate([dv, d_edge], axis=0)
+    x_parts = summands(normed, late_x)
+    d_bc_got, x_parts = lax.optimization_barrier((d_bc_got, x_parts))
+    late_shared, shared_sums = shared(
+        team.reshape(1), d_bc_got, conv, v, dr, flags, edge_flags, taps_shared
+    )
+    late_sum = jnp.concatenate(
+        [jnp.sum(p.astype(F32), axis=0) for p in (x_parts, summands(normed, late_shared))], axis=1
+    )
 
     ahead = MATRIX_MOMENTUM * momentum_block.astype(F32)
     late_new = (ahead[:, EG:IN_COLS] + late_sum).astype(BF16)
@@ -1378,6 +1384,7 @@
     sums_block = jnp.concatenate([early_sum[:, :EG], late_sum, early_sum[:, EG:]], axis=1)
     x_all = lax.all_gather(momenta, TEAM + ROWS).reshape(G, D, BLOCK)
 
+    late = jnp.concatenate([late_x, late_shared], axis=1)
     late_back = lax.ppermute(
         late[TOKENS:], "x", [(s, s - 1) for s in range(1, lax.axis_size("x"))]
     )
@@ -1462,15 +1469,12 @@
             in_grad, in_momentum_new, out_grad, out_momentum_new,
         )
     )
-    steps = solve(first, x_all, pick)
+    own_steps, other_steps = solve(first, x_all, pick)
     d_normed = lax.psum_scatter(d_normed_part, TEAM, scatter_dimension=0, tiled=True)
     mixed = lax.psum_scatter(mixed_part, TEAM, scatter_dimension=0, tiled=True)
     block_output, input_grad = finish(hidden, cotangent, d_normed, mixed, norm_gain[None, :])
 
-    own_steps = lax.dynamic_slice_in_dim(steps, ci * count, count, 1)
-    got_steps = lax.ppermute(
-        lax.dynamic_slice_in_dim(steps, (1 - ci) * count, count, 1), "c", swap
-    )
+    got_steps = lax.ppermute(other_steps, "c", swap)
     both = jnp.concatenate(
         [
             jnp.where(first, own_steps, got_steps),

time: 461 us -> 455 us (0.987)
  waiting for transfers between devices: 101 us -> 85 us
  starting transfers between devices: 73.9 us -> 80.5 us
    all_to_all x1 -> x2, waiting for transfers between devices: 25.2 us -> 8.61 us  [summands(): lax.all_to_all(part.reshape(16, D // 16, part.shape[1]), ROWS, 0, 0, tile...]
    all_to_all x1 -> x2, starting transfers between devices: 9.66 us -> 14 us  [summands(): lax.all_to_all(part.reshape(16, D // 16, part.shape[1]), ROWS, 0, 0, tile...]
    dot_general x3 -> x4, matrix products: 16.6 us -> 19.3 us  [dot(): lax.dot_general(a.astype(BF16), b.astype(BF16), (dims, ((), ())), preferr...]
    unnamed x196 -> x191, local copies, waits for them, and re-layouts: 28.1 us -> 27.6 us
  transfers between devices with their start and end apart: 34 -> 35, of which waited for: 16 -> 19; matrix products, arithmetic and copies ran while one was open for 11% -> 11% of each run, Pallas kernels for 26% -> 26%
where the time goes in v2:
time: 455 us; the launch traced here: 448 us
  Pallas kernels  130 us (29%)
  waiting for transfers between devices  85 us (19%)
  starting transfers between devices  80.5 us (18%)
  blocking collectives  53.8 us (12%)
  local copies, waits for them, and re-layouts  45.4 us (10%)
  matrix products  19.3 us (4%)
  other arithmetic  18.5 us (4%)
  between operations  15.7 us (3%)
    pallas_call x1, Pallas kernels, solve(): pl.pallas_call(solve_kernel, out_shape=[shaped(pieces, pick.shape[0] // 2...  73.7 us
    unnamed x191, local copies, waits for them, and re-layouts  27.6 us
    all_gather x1, waiting for transfers between devices, local(): x_all = lax.all_gather(momenta, TEAM + ROWS).reshape(G, D, BLOCK)  25.4 us
    all_gather x1, blocking collectives, local(): vector = lax.all_gather(vector, TEAM).reshape(G, -1)  21.9 us
    dot_general x4, matrix products, dot(): lax.dot_general(a.astype(BF16), b.astype(BF16), (dims, ((), ())), preferr...  19.3 us
    all_gather x1, blocking collectives, local(): vector = jnp.sum(lax.all_gather(vector, ROWS), axis=0)  18 us
    ppermute x1, starting transfers between devices, local(): got_steps = lax.ppermute(other_steps, 'c', swap)  16.2 us
    all_to_all x2, starting transfers between devices, summands(): lax.all_to_all(part.reshape(16, D // 16, part.shape[1]), ROWS, 0, 0, tile...  14 us
  transfers between devices with their start and end apart: 35, of which 19 were waited for; matrix products, arithmetic and copies ran while one was open for 11% of the time, Pallas kernels for 26%

profile of v2, /device:TPU:1, one launch (start us, length us, event | category | flops | bytes accessed | tf_op | source)
XLA Modules:
  0.0 448.3 jit_solution(5857805029198230633)
XLA Ops:
  10.9 13.9 %all_to_all.25 = bf16[8,12,1536]{2,1,0:T(8,128)(2,1)S(1)} all-to-all(bf16[8,12,1536]{2,1,0:T(8,128)(2,1)S(1)} %bitcast.140), channel_id=1, replica_groups=mesh['z'=4,'x'=4,'y'=4,'c'=2] {'y','c'}, dimensions={0} | all-to-all | bytes 589824 | tf_op jit(solution)/shard_map/all_to_all | solution.py:1243
  31.4 5.5 %all-to-all-start.1 = ((bf16[8,12,1280]{2,1,0:T(8,128)(2,1)}), bf16[8,12,1280]{2,1,0:T(8,128)(2,1)S(1)}, u32[]{:S(2)}, u32[]{:S(2)}) async-start(bf16[8,12,1280]{2,1,0:T(8,128)(2,1)} %bitcast.2), calls=%async_computation.1 | async-start | bytes 655360 | tf_op jit(solution)/shard_map/all_to_all | solution.py:1248
  37.1 14.0 %all-to-all-done.1 = bf16[8,12,1280]{2,1,0:T(8,128)(2,1)S(1)} async-done(((bf16[8,12,1280]{2,1,0:T(8,128)(2,1)}), bf16[8,12,1280]{2,1,0:T(8,128)(2,1)S(1)}, u32[]{:S(2)}, u32[]{:S(2)}) %all-to-all-start.1) | async-done | bytes 245792 | tf_op jit(solution)/shard_map/all_to_all | solution.py:1248
  71.3 6.1 %collective-permute-done.6 = bf16[128,1536]{1,0:T(8,128)(2,1)} collective-permute-done((bf16[128,1536]{1,0:T(8,128)(2,1)S(1)}, bf16[128,1536]{1,0:T(8,128)(2,1)}, u32[]{:S(2)}, u32[]{:S(2)}) %collective-permute-start.6) | collective-permute-done | bytes 393248 | tf_op jit(solution)/shard_map/ppermute | solution.py:1188
  84.9 9.5 %project.1 = (bf16[1040,1536]{1,0:T(8,128)(2,1)S(1)}, f32[1040,384]{1,0:T(8,128)S(1)}, f32[1040,640]{1,0:T(8,128)S(1)}, f32[1040,128]{1,0:T(8,128)S(1)}) custom-call(s32[2]{0:T(128)S(1)} %pad_add_fusion.core_ref, bf16[4,128,1664]{2,1,0:T(8,128)(2,1)S(1)} %copy-done.17, bf16[4,128,1664]{2,1,0:T(8,128)(2,1)} %collective-permute-done.3.other_ref, ...), custom_call_target="tpu_custom_call" | custom-call | flops 3680501760 | bytes 16777216 | tf_op jit(solution)/shard_map/project/pallas_call | solution.py:836
  94.5 8.6 %forward.1 = (f32[1024,640]{1,0:T(8,128)S(1)}, f32[1024,128]{1,0:T(8,128)S(1)}, f32[1024,128]{1,0:T(8,128)S(1)}, f32[1024,384]{1,0:T(8,128)S(1)}, f32[8,128,384]...) custom-call(f32[1040,640]{1,0:T(8,128)S(1)} %get-tuple-element.101.v_ref.before_ref.refs_2, ...), custom_call_target="tpu_custom_call" | custom-call | flops 3221225472 | bytes 14680064 | tf_op jit(solution)/shard_map/forward/pallas_call | solution.py:906
  107.1 4.4 collective-permute-start.11
  112.8 4.7 %incoming.1 = (bf16[1024,1536]{1,0:T(8,128)(2,1)S(1)}, f32[1024,384]{1,0:T(8,128)S(1)}) custom-call(s32[2]{0:T(128)S(1)} %pad_add_fusion.core_ref, bf16[4,128,1536]{2,1,0:T(8,128)(2,1)} %pad_maximum_fusion.1.own_ref, bf16[4,128,1536]{2,1,0:T(8,128)(2,1)} %collective-permute-done.9.other_ref, bf16[1536,1536]{1,0:T(8,128)(2,1)S(1)} %bitcast.108), custom_call_target="tpu_custom_call" | custom-call | flops 1207959552 | bytes 9437184 | tf_op jit(solution)/shard_map/incoming/pallas_call | solution.py:868
  129.2 4.2 gate.1
  136.4 5.1 %early.1 = bf16[1536,768]{1,0:T(8,128)(2,1)S(1)} custom-call(bf16[1040,1536]{1,0:T(8,128)(2,1)S(1)} %get-tuple-element.124.normed_ref, bf16[1024,1536]{1,0:T(8,128)(2,1)S(1)} %get-tuple-element.125.q_ref, bf16[1024,384]{1,0:T(8,128)(2,1)S(1)} %get-tuple-element.154.dz_ref, bf16[1024,384]{1,0:T(8,128)(2,1)S(1)} %get-tuple-element.157.gated_ref), custom_call_target="tpu_custom_call" | custom-call | flops 2415919104 | bytes 13631488 | tf_op jit(solution)/shard_map/early/pallas_call | solution.py:888
  154.2 5.8 %inner.1 = (f32[1024,384]{1,0:T(8,128)S(1)}, f32[1024,256]{1,0:T(8,128)S(1)}) custom-call(f32[1024,384]{1,0:T(8,128)S(1)} %copy-done.21, f32[1024,640]{1,0:T(8,128)S(1)} %copy-done.1, f32[1024,128]{1,0:T(8,128)S(1)} %copy-done.31, f32[1024,128]{1,0:T(8,128)S(1)} %copy-done.9, f32[1024,128]{1,0:T(8,128)S(1)} %pad.44.flags_ref.refs_7_, f32[8,128]{1,0:T(8,128)S(1)} %bitcast.117), custom_call_target="tpu_custom_call" | custom-call | flops 3221225472 | bytes 9437184 | tf_op jit(solution)/shard_map/inner/pallas_call | solution.py:991
  161.7 10.5 %backward.1 = (bf16[1024,384]{1,0:T(8,128)(2,1)S(1)}, bf16[16,384]{1,0:T(8,128)(2,1)S(1)}, f32[128,1024]{1,0:T(8,128)S(1)}, f32[128,1024]{1,0:T(8,128)S(1)}, f32...) custom-call(s32[2]{0:T(128)S(1)} %pad_add_fusion.core_ref, ...), custom_call_target="tpu_custom_call" | custom-call | flops 1610612736 | bytes 20971520 | tf_op jit(solution)/shard_map/backward/pallas_call | solution.py:1010
  175.6 8.3 %all-to-all-start.2 = ((bf16[16,96,384]{2,1,0:T(8,128)(2,1)}), bf16[16,96,384]{2,1,0:T(8,128)(2,1)}, u32[]{:S(2)}, u32[]{:S(2)}) async-start(bf16[16,96,384]{2,1,0:T(8,128)(2,1)} %bitcast.126), calls=%async_computation.2 | async-start | bytes 2359296 | tf_op jit(solution)/shard_map/all_to_all | solution.py:1199
  212.6 5.7 %all-to-all-start.3 = ((bf16[16,96,128]{2,1,0:T(8,128)(2,1)}), bf16[16,96,128]{2,1,0:T(8,128)(2,1)S(1)}, u32[]{:S(2)}, u32[]{:S(2)}) async-start(bf16[16,96,128]{2,1,0:T(8,128)(2,1)} %bitcast.40), calls=%async_computation.3 | async-start | bytes 786432 | tf_op jit(solution)/shard_map/all_to_all | solution.py:1199
  220.0 7.5 %all-to-all-done.3 = bf16[16,96,128]{2,1,0:T(8,128)(2,1)S(1)} async-done(((bf16[16,96,128]{2,1,0:T(8,128)(2,1)}), bf16[16,96,128]{2,1,0:T(8,128)(2,1)S(1)}, u32[]{:S(2)}, u32[]{:S(2)}) %all-to-all-start.3) | async-done | bytes 393248 | tf_op jit(solution)/shard_map/all_to_all | solution.py:1199
  241.4 8.4 %multiply_reduce_fusion = (f32[1536]{0:T(1024)S(1)}, f32[1024,1536]{1,0:T(8,128)}) fusion(bf16[1040,1536]{1,0:T(8,128)(2,1)} %copy-done.13, bf16[1536,6]{1,0:T(8,128)(2,1)S(1)} %slice-done.4, bf16[1536,32]{1,0:T(8,128)(2,1)} %constant_dynamic-slice_fusion, bf16[1536,768]{1,0:T(8,128)(2,1)S(1)} %slice-done.3, bf16[896]{0:T(1024)(128)(2,1)S(1)} %pad.64.clone, ...), kind=kOutput, calls=%fused_computation.1 | convolution fusion | flops 2839804416 | bytes 13756160 | tf_op jit(solution)/shard_map/dot_general | solution.py:58
  249.8 18.0 %all_gather.21 = f32[16,32,128]{2,1,0:T(8,128)S(1)} all-gather(f32[1,32,128]{2,1,0:T(8,128)S(1)} %pad_bitcast_fusion), channel_id=1, replica_groups=mesh['z'=4,'x'=4,'y'=4,'c'=2] {'z','x'}, dimensions={0}, use_global_device_ids=true | all-gather | bytes 278528 | tf_op jit(solution)/shard_map/all_gather | solution.py:1427
  267.9 21.9 %all-gather.1 = f32[256,128]{1,0:T(8,128)S(1)} all-gather(f32[32,128]{1,0:T(8,128)S(1)} %reduce_sum.48), channel_id=3, replica_groups=mesh['z'=4,'x'=4,'y'=4,'c'=2] {'y','c'}, dimensions={0}, use_global_device_ids=true | all-gather | bytes 147456 | tf_op jit(solution)/shard_map/all_gather | solution.py:1428
  292.2 4.6 %all-to-all-start.4 = ((f32[8,12,1280]{2,1,0:T(8,128)}), f32[8,12,1280]{2,1,0:T(8,128)S(1)}, u32[]{:S(2)}, u32[]{:S(2)}) async-start(f32[8,12,1280]{2,1,0:T(8,128)} %reshape.290), calls=%async_computation.5 | async-start | bytes 1310720 | tf_op jit(solution)/shard_map/all_to_all | solution.py:1449
  296.8 5.8 %fusion.13 = f32[1024,1536]{1,0:T(8,128)} fusion(bf16[1024,384]{1,0:T(8,128)(2,1)S(1)} %copy-done.12, bf16[1536,1536]{1,0:T(8,128)(2,1)} %all-gather.5.cloned.1.call-done.w_ref), kind=kOutput, calls=%fused_computation.22 | convolution fusion | flops 1207959552 | bytes 8257536 | tf_op jit(solution)/shard_map/dot_general | solution.py:58
  302.6 12.4 %all-to-all-done.4 = f32[8,12,1280]{2,1,0:T(8,128)S(1)} async-done(((f32[8,12,1280]{2,1,0:T(8,128)}), f32[8,12,1280]{2,1,0:T(8,128)S(1)}, u32[]{:S(2)}, u32[]{:S(2)}) %all-to-all-start.4) | async-done | bytes 491552 | tf_op jit(solution)/shard_map/all_to_all | solution.py:1449
  317.6 25.4 %all-gather.7.cloned.1.call-done = bf16[12288,1280]{1,0:T(8,128)(2,1)} async-done(((bf16[96,1280]{1,0:T(8,128)(2,1)}), bf16[12288,1280]{1,0:T(8,128)(2,1)}) %all-gather.7.cloned.1.call-update) | async-done | bytes 31457296 | tf_op jit(solution)/shard_map/all_gather | solution.py:1385
  343.6 73.7 %solve.1 = (f32[8,12,896]{2,1,0:T(8,128)}, f32[8,12,896]{2,1,0:T(8,128)}) custom-call(s32[1]{0:T(128)} %bitcast.47.which_ref, bf16[8,1536,1280]{2,1,0:T(8,128)(2,1)} %bitcast.169, f32[24,1536]{1,0:T(8,128)} %fusion.20.pick_ref), custom_call_target="tpu_custom_call" | custom-call | flops 72477573120 | bytes 46137344 | tf_op jit(solution)/shard_map/solve/pallas_call | solution.py:1131
  417.4 16.2 %collective-permute-start.25 = (f32[8,12,896]{2,1,0:T(8,128)}, f32[8,12,896]{2,1,0:T(8,128)S(1)}, u32[]{:S(2)}, u32[]{:S(2)}) collective-permute-start(f32[8,12,896]{2,1,0:T(8,128)} %get-tuple-element.171), channel_id=1, source_target_pairs={{0,1},{1,0},{2,3},{3,2},{4,5},{5,4},{6,7},{7,6},{8,9},{9,8},{10,11... | collective-permute-start | bytes 1032200 | tf_op jit(solution)/shard_map/ppermute | solution.py:1477
  (435 shorter events, 132.5 us)
Async XLA Ops:
  7.2 74.0 %all-gather.5.cloned.1.call-start = ((), (), s32[]{:S(2)}) async-start(), calls=%async_computation.8 | async-start | bytes 5013504 | tf_op jit(solution)/shard_map/all_gather | solution.py:1244
  25.8 26.1 %collective-permute-start = (bf16[128,1664]{1,0:T(8,128)(2,1)S(1)}, bf16[128,1664]{1,0:T(8,128)(2,1)S(1)}, u32[]{:S(2)}, u32[]{:S(2)}) collective-permute-start(bf16[128,1664]{1,0:T(8,128)(2,1)S(1)} %fusion.16), channel_id=1, source_target_pairs={{0,2},{2,4},{4,6},{6,0},{1,3},{3,5},{5,7},{7,1},{8,10},{10,12},{12... | collective-permute-start | bytes 1277960 | tf_op jit(solution)/shard_map/ppermute | solution.py:1188
  26.2 25.7 %collective-permute-start.1 = (bf16[128,1664]{1,0:T(8,128)(2,1)S(1)}, bf16[128,1664]{1,0:T(8,128)(2,1)S(1)}, u32[]{:S(2)}, u32[]{:S(2)}) collective-permute-start(bf16[128,1664]{1,0:T(8,128)(2,1)S(1)} %fusion.16), channel_id=1, source_target_pairs={{0,4},{2,6},{4,0},{6,2},{1,5},{3,7},{5,1},{7,3},{8,12},{10,14},{12... | collective-permute-start | bytes 1277960 | tf_op jit(solution)/shard_map/ppermute | solution.py:1188
  27.9 23.9 %collective-permute-start.2 = (bf16[128,1664]{1,0:T(8,128)(2,1)S(1)}, bf16[128,1664]{1,0:T(8,128)(2,1)S(1)}, u32[]{:S(2)}, u32[]{:S(2)}) collective-permute-start(bf16[128,1664]{1,0:T(8,128)(2,1)S(1)} %fusion.16), channel_id=1, source_target_pairs={{0,6},{2,0},{4,2},{6,4},{1,7},{3,1},{5,3},{7,5},{8,14},{10,8},{12,... | collective-permute-start | bytes 1277960 | tf_op jit(solution)/shard_map/ppermute | solution.py:1188
  31.4 19.8 %all-to-all-start.1 = ((bf16[8,12,1280]{2,1,0:T(8,128)(2,1)}), bf16[8,12,1280]{2,1,0:T(8,128)(2,1)S(1)}, u32[]{:S(2)}, u32[]{:S(2)}) async-start(bf16[8,12,1280]{2,1,0:T(8,128)(2,1)} %bitcast.2), calls=%async_computation.1 | async-start | bytes 655360 | tf_op jit(solution)/shard_map/all_to_all | solution.py:1248
  36.9 191.9 %reduce-scatter.4.cloned.1.call-start = ((), (), s32[]{:S(2)}) async-start(), calls=%async_computation.9 | async-start | bytes 2506752 | tf_op jit(solution)/shard_map/reduce_scatter | solution.py:1346
  55.4 15.9 %collective-permute-start.5 = (bf16[128,1536]{1,0:T(8,128)(2,1)S(1)}, bf16[128,1536]{1,0:T(8,128)(2,1)}, u32[]{:S(2)}, u32[]{:S(2)}) collective-permute-start(bf16[128,1536]{1,0:T(8,128)(2,1)S(1)} %copy-done.51), channel_id=1, source_target_pairs={{0,2},{2,4},{4,6},{6,0},{1,3},{3,5},{5,7},{7,1},{8,10},{10,12},{12... | collective-permute-start | bytes 1179656 | tf_op jit(solution)/shard_map/ppermute | solution.py:1188
  56.2 21.2 %collective-permute-start.6 = (bf16[128,1536]{1,0:T(8,128)(2,1)S(1)}, bf16[128,1536]{1,0:T(8,128)(2,1)}, u32[]{:S(2)}, u32[]{:S(2)}) collective-permute-start(bf16[128,1536]{1,0:T(8,128)(2,1)S(1)} %copy-done.51), channel_id=1, source_target_pairs={{0,4},{2,6},{4,0},{6,2},{1,5},{3,7},{5,1},{7,3},{8,12},{10,14},{12... | collective-permute-start | bytes 1179656 | tf_op jit(solution)/shard_map/ppermute | solution.py:1188
  59.7 17.8 %collective-permute-start.7 = (bf16[128,1536]{1,0:T(8,128)(2,1)S(1)}, bf16[128,1536]{1,0:T(8,128)(2,1)}, u32[]{:S(2)}, u32[]{:S(2)}) collective-permute-start(bf16[128,1536]{1,0:T(8,128)(2,1)S(1)} %copy-done.51), channel_id=1, source_target_pairs={{0,6},{2,0},{4,2},{6,4},{1,7},{3,1},{5,3},{7,5},{8,14},{10,8},{12,... | collective-permute-start | bytes 1179656 | tf_op jit(solution)/shard_map/ppermute | solution.py:1188
  80.1 32.7 %collective-permute-start.9 = (bf16[4,128,1536]{2,1,0:T(8,128)(2,1)}, bf16[4,128,1536]{2,1,0:T(8,128)(2,1)}, u32[]{:S(2)}, u32[]{:S(2)}) collective-permute-start(bf16[4,128,1536]{2,1,0:T(8,128)(2,1)} %pad_maximum_fusion.1.own_ref), channel_id=1, source_target_pairs={{0,1},{1,0},{2,3},{3,2},{4,5},{5,4},{6,7},{7,6},{8,9},{9,8},{10,11... | collective-permute-start | bytes 4718600 | tf_op jit(solution)/shard_map/ppermute | solution.py:1331
  103.9 13.6 %collective-permute-start.10 = (f32[136,384]{1,0:T(8,128)S(1)}, f32[136,384]{1,0:T(8,128)S(1)}, u32[]{:S(2)}, u32[]{:S(2)}) collective-permute-start(f32[136,384]{1,0:T(8,128)S(1)} %get-tuple-element.117.final_ref), channel_id=1, source_target_pairs={{0,8},{8,16},{16,24},{1,9},{9,17},{17,25},{2,10},{10,18},{18,26},{... | collective-permute-start | bytes 626696 | tf_op jit(solution)/shard_map/ppermute | solution.py:1152
  107.1 10.5 %collective-permute-start.11 = (f32[136,384]{1,0:T(8,128)S(1)}, f32[136,384]{1,0:T(8,128)S(1)}, u32[]{:S(2)}, u32[]{:S(2)}) collective-permute-start(f32[136,384]{1,0:T(8,128)S(1)} %get-tuple-element.117.final_ref), channel_id=1, source_target_pairs={{0,16},{8,24},{1,17},{9,25},{2,18},{10,26},{3,19},{11,27},{4,20},{... | collective-permute-start | bytes 626696 | tf_op jit(solution)/shard_map/ppermute | solution.py:1152
  111.4 7.9 %collective-permute-start.12 = (f32[136,384]{1,0:T(8,128)S(1)}, f32[136,384]{1,0:T(8,128)S(1)}, u32[]{:S(2)}, u32[]{:S(2)}) collective-permute-start(f32[136,384]{1,0:T(8,128)S(1)} %get-tuple-element.117.final_ref), channel_id=1, source_target_pairs={{0,24},{1,25},{2,26},{3,27},{4,28},{5,29},{6,30},{7,31},{32,56},{3... | collective-permute-start | bytes 626696 | tf_op jit(solution)/shard_map/ppermute | solution.py:1152
  144.7 15.4 %collective-permute-start.17 = (f32[136,384]{1,0:T(8,128)}, f32[136,384]{1,0:T(8,128)S(1)}, u32[]{:S(2)}, u32[]{:S(2)}) collective-permute-start(f32[136,384]{1,0:T(8,128)} %copy-done.46), channel_id=1, source_target_pairs={{8,0},{16,8},{24,16},{9,1},{17,9},{25,17},{10,2},{18,10},{26,18},{... | collective-permute-start | bytes 626696 | tf_op jit(solution)/shard_map/ppermute | solution.py:1152
  146.4 13.7 %collective-permute-start.18 = (f32[136,384]{1,0:T(8,128)}, f32[136,384]{1,0:T(8,128)S(1)}, u32[]{:S(2)}, u32[]{:S(2)}) collective-permute-start(f32[136,384]{1,0:T(8,128)} %copy-done.46), channel_id=1, source_target_pairs={{16,0},{24,8},{17,1},{25,9},{18,2},{26,10},{19,3},{27,11},{20,4},{... | collective-permute-start | bytes 626696 | tf_op jit(solution)/shard_map/ppermute | solution.py:1152
  147.7 13.9 %collective-permute-start.19 = (f32[136,384]{1,0:T(8,128)}, f32[136,384]{1,0:T(8,128)S(1)}, u32[]{:S(2)}, u32[]{:S(2)}) collective-permute-start(f32[136,384]{1,0:T(8,128)} %copy-done.46), channel_id=1, source_target_pairs={{24,0},{25,1},{26,2},{27,3},{28,4},{29,5},{30,6},{31,7},{56,32},{5... | collective-permute-start | bytes 626696 | tf_op jit(solution)/shard_map/ppermute | solution.py:1152
  175.6 26.0 %all-to-all-start.2 = ((bf16[16,96,384]{2,1,0:T(8,128)(2,1)}), bf16[16,96,384]{2,1,0:T(8,128)(2,1)}, u32[]{:S(2)}, u32[]{:S(2)}) async-start(bf16[16,96,384]{2,1,0:T(8,128)(2,1)} %bitcast.126), calls=%async_computation.2 | async-start | bytes 2359296 | tf_op jit(solution)/shard_map/all_to_all | solution.py:1199
  190.9 8.2 %collective-permute-start.22 = (f32[32,1024]{1,0:T(8,128)S(1)}, f32[32,1024]{1,0:T(8,128)S(1)}, u32[]{:S(2)}, u32[]{:S(2)}) collective-permute-start(f32[32,1024]{1,0:T(8,128)S(1)} %get-tuple-element.193), channel_id=1, source_target_pairs={{0,4},{2,6},{4,0},{6,2},{1,5},{3,7},{5,1},{7,3},{8,12},{10,14},{12... | collective-permute-start | bytes 393224 | tf_op jit(solution)/shard_map/ppermute | solution.py:1360
  212.6 14.9 %all-to-all-start.3 = ((bf16[16,96,128]{2,1,0:T(8,128)(2,1)}), bf16[16,96,128]{2,1,0:T(8,128)(2,1)S(1)}, u32[]{:S(2)}, u32[]{:S(2)}) async-start(bf16[16,96,128]{2,1,0:T(8,128)(2,1)} %bitcast.40), calls=%async_computation.3 | async-start | bytes 786432 | tf_op jit(solution)/shard_map/all_to_all | solution.py:1199
  218.3 124.7 %all-gather.7.cloned.1.call-start = ((), (), s32[]{:S(2)}) async-start(), calls=%async_computation.12 | async-start | bytes 31703040 | tf_op jit(solution)/shard_map/all_gather | solution.py:1385
  292.2 22.8 %all-to-all-start.4 = ((f32[8,12,1280]{2,1,0:T(8,128)}), f32[8,12,1280]{2,1,0:T(8,128)S(1)}, u32[]{:S(2)}, u32[]{:S(2)}) async-start(f32[8,12,1280]{2,1,0:T(8,128)} %reshape.290), calls=%async_computation.5 | async-start | bytes 1310720 | tf_op jit(solution)/shard_map/all_to_all | solution.py:1449
  296.8 142.1 %reduce-scatter.6.cloned.1.call-start = ((), (), s32[]{:S(2)}) async-start(), calls=%async_computation.10 | async-start | bytes 7077888 | tf_op jit(solution)/shard_map/reduce_scatter | solution.py:1473
  343.1 95.8 %reduce-scatter.8.cloned.1.call-start = ((), (), s32[]{:S(2)}) async-start(), calls=%async_computation.11 | async-start | bytes 7077888 | tf_op jit(solution)/shard_map/reduce_scatter | solution.py:1474
  417.4 17.9 %collective-permute-start.25 = (f32[8,12,896]{2,1,0:T(8,128)}, f32[8,12,896]{2,1,0:T(8,128)S(1)}, u32[]{:S(2)}, u32[]{:S(2)}) collective-permute-start(f32[8,12,896]{2,1,0:T(8,128)} %get-tuple-element.171), channel_id=1, source_target_pairs={{0,1},{1,0},{2,3},{3,2},{4,5},{5,4},{6,7},{7,6},{8,9},{9,8},{10,11... | collective-permute-start | bytes 1032200 | tf_op jit(solution)/shard_map/ppermute | solution.py:1477
  (96 other events, 846.7 us)
Sparse Core Ops, SparseCore 0:
  25.7 54.6 all-gather.4
  144.8 83.9 reduce-scatter.3
  232.2 110.7 all-gather.6
  345.3 41.0 reduce-scatter.5
  388.6 42.1 reduce-scatter.7
